TPU v7x, 512 devices: a whole 4x8x8 slice. The times are simulated.
512 devices in a mesh: ka: 8 (over z_lo, core), pair: 64 (over y, z_hi, x).
Axes of the slice: x: 4, y: 8, z: 8 (z_hi: 2, z_lo: 4; z = z_hi * 4 + z_lo), core: 2. Of those that a mesh axis runs over, the one named last changes fastest.
Arguments:
- cond_orbitals: bfloat16 [8, 2048, 8192], P('ka', 'pair'), may hold values from -6 to 6
- cond_energy: float32 [8, 8192], P('ka', 'pair'), may hold values from 0.5 to 8
- val_orbitals: bfloat16 [512, 2048], P(('ka', 'pair')), may hold values from -6 to 6
- val_energy: bfloat16 [512], P(('ka', 'pair')), may hold values from -8 to -0.5
- val_slots: int32 [8, 64, 16], P('ka', 'pair'), may hold values from 0 to 511
- owner_count: int32 [8, 64], P('ka', 'pair'), may hold values from 1 to 16, as said below
Outputs:
- response: float32 [8, 2048, 512], P('ka', 'pair')
Inputs may be any that keep to these rules, and one draw needn't show every extreme that they name: `owner_count`: in every lane some owner has exactly 16 live slots.
All inputs are finite; a program needn't handle non-finite values.
Results may differ from a plain program's by a relative error of at most 0.0047.
The roundings to bfloat16 on the way count: a program that leaves them out, or rounds other values in their place, can miss the bound.
Values may be sent and summed in bfloat16 or wider, within the bound.
No kernel may reach another device: no remote copies, remote signals or barrier semaphores. Data moves between devices by JAX's collectives and lax.ppermute only.
A program may use at most 64 MiB of HBM per device.

v0:
```python
import jax
import jax.numpy as jnp
from jax import lax
from jax.sharding import PartitionSpec as P

BC = 128
GA = 16
GB = 128
WIN = 512
SLOTS = 16


def cosine_table(length):
    freq = lax.iota(jnp.float32, length)[:, None]
    point = lax.iota(jnp.float32, length)[None, :]
    factor = jnp.where(freq == 0, jnp.sqrt(1.0 / length), jnp.sqrt(2.0 / length))
    return (factor * jnp.cos(jnp.pi * (point + 0.5) * freq / length)).astype(jnp.bfloat16)


def owner_terms(picked, e_pick, live, cond_block, e_cond, table_a, table_b):
    slots = picked.shape[0]
    pair_real = (
        picked[:, None, :].astype(jnp.float32) * cond_block[None].astype(jnp.float32)
    ).astype(jnp.bfloat16)
    count = slots * cond_block.shape[0]
    rows = pair_real.reshape(count * GA, GB)
    first = jnp.dot(rows, table_b.T, preferred_element_type=jnp.float32).astype(jnp.bfloat16)
    first = first.reshape(count, GA, GB)
    moved = jnp.einsum("ja,pak->pjk", table_a, first, preferred_element_type=jnp.float32)
    moved = moved.astype(jnp.bfloat16).reshape(count, GA * GB)
    weight = live[:, None] * 2.0 / (e_cond[None, :] - e_pick[:, None])
    weighted = (moved[:, :WIN].astype(jnp.float32) * weight.reshape(count, 1)).astype(jnp.bfloat16)
    return (moved, weighted)


def shards(cond_orbitals, cond_energy, val_orbitals, val_energy, val_slots, owner_count):
    cond_block = lax.all_to_all(cond_orbitals, "pair", split_axis=2, concat_axis=1, tiled=True)[0].T
    all_orb, all_energy = (
        lax.all_gather(val_orbitals, ("ka", "pair"), axis=0, tiled=True),
        lax.all_gather(val_energy, ("ka", "pair"), axis=0, tiled=True),
    )
    slots = val_slots[0, 0]
    picked = jnp.take(all_orb, slots, axis=0)
    e_pick = jnp.take(all_energy, slots).astype(jnp.float32)
    live = (lax.iota(jnp.int32, slots.shape[0]) < owner_count[0, 0]).astype(jnp.float32)
    moved, weighted = owner_terms(
        picked, e_pick, live, cond_block, cond_energy[0], cosine_table(GA), cosine_table(GB)
    )
    owners = lax.axis_size("pair")
    grid_len = moved.shape[1]
    own_rows = grid_len // owners
    summed = lax.psum(
        lax.dot_general(
            moved, weighted, (((0,), (0,)), ((), ())), preferred_element_type=jnp.float32
        ),
        "pair",
    )
    mine = lax.dynamic_slice_in_dim(summed, lax.axis_index("pair") * own_rows, own_rows, 0)
    scale = 2.0 / (SLOTS * BC * owners)
    return (mine * scale)[None]


def solution(mesh):
    return jax.shard_map(
        shards,
        mesh=mesh,
        in_specs=(
            P("ka", "pair", None),
            P("ka", "pair"),
            P(("ka", "pair"), None),
            P(("ka", "pair")),
            P("ka", "pair", None),
            P("ka", "pair"),
        ),
        out_specs=P("ka", "pair", None),
        check_vma=False,
    )
```

profile of v0, /device:TPU:2, one launch (start us, length us, event | category | flops | bytes accessed | tf_op | source)
XLA Modules:
  0.0 2326.5 jit_solution(4205094719186806137)
XLA Ops:
  6.5 0.0 copy-start.1
  6.5 0.0 copy-start
  6.5 0.0 all-gather.3.cloned.1.call-start
  6.5 0.7 all-gather.3.cloned.1.call-update
  7.3 8.6 copy.18
  15.9 0.5 broadcast.173
  16.4 45.2 %reduce = bf16[8192,32]{1,0:T(8,128)(2,1)S(1)} reduce(bf16[8192,1,32]{2,1,0:T(2,128)(2,1)} %bitcast.45, bf16[]{:T(256)} %broadcast.173), dimensions={1}, to_apply=%bitcast.34.reduce_sub_computation | reduce | bytes 1048578
  61.6 2.8 reshape.162
  64.4 19.1 all-to-all-start
  83.5 0.0 all-reduce.3.cloned.1.call-start
  84.9 0.1 dynamic-update-slice
  85.0 103.8 %all-reduce = bf16[512]{0:T(512)(128)(2,1)S(1)} all-reduce(bf16[512]{0:T(512)(128)(2,1)S(1)} %dynamic-update-slice), channel_id=1, replica_groups=mesh['ka'=8,'pair'=64] {'ka','pair'}, use_global_device_ids=true, to_apply=%add | all-reduce | flops 512 | bytes 2048
  188.8 0.0 copy-done.1
  188.8 0.7 gather_fusion.1
  189.5 0.0 copy-done
  189.5 0.1 divide_bitcast_fusion
  189.6 0.0 all-to-all-done
  189.6 7.2 reshape.163
  196.8 8.0 copy.19
  204.8 0.1 convert_bitcast_fusion
  204.9 0.2 copy.23
  205.1 0.6 copy.20
  205.7 0.3 copy.21
  206.0 1193.1 %all-gather.3.cloned.1.call-done = bf16[512,1,2048]{2,1,0:T(2,128)(2,1)} async-done(((bf16[1,1,2048]{2,1,0:T(2,128)(2,1)}), bf16[512,1,2048]{2,1,0:T(2,128)(2,1)}) %all-gather.3.cloned.1.call-update) | async-done | bytes 2097168 | tf_op jit(solution)/shard_map/all_gather | solution.py:39
  1399.1 3.5 copy.28
  1402.6 0.6 gather_fusion
  1403.2 0.1 select_convert_fusion
  1403.3 5.4 multiply_convert_fusion
  1408.6 13.5 convert_element_type.68
  1422.1 5.9 convolution_convert_fusion
  1428.0 5.6 convolution_convert_fusion.1
  1433.7 10.9 copy.27
  1444.5 10.6 fusion
  1455.1 0.0 all-reduce.3.cloned.1.call-update
  1455.1 863.1 %all-reduce.3.cloned.1.call-done = f32[2048,512]{1,0:T(8,128)} async-done(((f32[2048,512]{1,0:T(8,128)}), f32[2048,512]{1,0:T(8,128)}) %all-reduce.3.cloned.1.call-update) | async-done | bytes 4194320 | tf_op jit(solution)/shard_map/psum | solution.py:52
  2318.2 1.5 multiply_bitcast_fusion
  (7 shorter events, 0.0 us)
Async XLA Ops:
  6.5 182.2 %copy-start.1 = (s32[1,1,16]{2,1,0:T(1,128)S(1)}, s32[1,1,16]{2,1,0:T(1,128)}, u32[]{:S(2)}) copy-start(s32[1,1,16]{2,1,0:T(1,128)} %param.10) | copy-start | bytes 196
  6.5 183.0 %copy-start = (f32[1,128]{1,0:T(1,128)S(1)}, f32[1,128]{1,0:T(1,128)}, u32[]{:S(2)}) copy-start(f32[1,128]{1,0:T(1,128)} %param.7) | copy-start | bytes 1540
  6.5 1392.6 %all-gather.3.cloned.1.call-start = ((), (), s32[]{:S(2)}) async-start(), calls=%async_computation.2 | async-start | bytes 4202496 | tf_op jit(solution)/shard_map/all_gather | solution.py:39
  64.4 125.2 %all-to-all-start = ((bf16[64,2,2048]{2,1,0:T(2,128)(2,1)}), bf16[64,2,2048]{2,1,0:T(2,128)(2,1)S(1)}, u32[]{:S(2)}, u32[]{:S(2)}) async-start(bf16[64,2,2048]{2,1,0:T(2,128)(2,1)} %reshape.162), calls=%async_computation | async-start | bytes 1048576 | tf_op jit(solution)/shard_map/all_to_all | solution.py:37
  83.5 2234.7 %all-reduce.3.cloned.1.call-start = ((), (), s32[]{:S(2)}) async-start(), calls=%async_computation.1 | async-start | bytes 8388608 | tf_op jit(solution)/shard_map/psum | solution.py:52
Sparse Core Ops, SparseCore 0:
  9.6 1389.4 all-gather.2
  1455.2 862.9 all-reduce.2
where the time goes:
time: 2330 us
  waiting for transfers between devices  2060 us (88%)
  blocking collectives  104 us (4%)
  local copies, waits for them, and re-layouts  57.4 us (2%)
  other arithmetic  52.3 us (2%)
    all_gather x1, waiting for transfers between devices, shards(): lax.all_gather(val_orbitals, ('ka', 'pair'), axis=0, tiled=True)  1190 us
    psum x1, waiting for transfers between devices, shards(): lax.psum(lax.dot_general(moved, weighted, (((0,), (0,)), ((), ())), prefe...  863 us
    unnamed x1, blocking collectives  104 us
  transfers between devices with their start and end apart: 3, of which 2 were waited for; matrix products, arithmetic and copies ran while one was open for 3% of the time, Pallas kernels for 0%

commit v1 on v0

v1 whole, which is shorter than its diff:
```python
import jax
import jax.numpy as jnp
from jax import lax
from jax.experimental import pallas as pl
from jax.experimental.pallas import tpu as pltpu
from jax.sharding import PartitionSpec as P

BC = 128
GA = 16
GB = 128
WIN = 512
SLOTS = 16
GRID = 2048
NC = 8192
N_KA = 8
N_PAIR = 64
OWN = GRID // N_PAIR
PAIRS = SLOTS * BC
BLOCK = OWN + GA + 8

f32 = jnp.float32
bf16 = jnp.bfloat16


def cosine_table(length):
    freq = lax.iota(jnp.float32, length)[:, None]
    point = lax.iota(jnp.float32, length)[None, :]
    factor = jnp.where(freq == 0, jnp.sqrt(1.0 / length), jnp.sqrt(2.0 / length))
    return (factor * jnp.cos(jnp.pi * (point + 0.5) * freq / length)).astype(jnp.bfloat16)


def vmem(count):
    return [pl.BlockSpec(memory_space=pltpu.VMEM)] * count


def params():
    return pltpu.CompilerParams(vmem_limit_bytes=48 * 2**20)


def pack_kernel(cond_ref, val_ref, energy_ref, out_ref):
    for d in range(N_PAIR):
        out_ref[d, :OWN, :] = cond_ref[:, d * BC:(d + 1) * BC]
        out_ref[d, OWN:OWN + GA, :] = val_ref[...]
        out_ref[d, OWN + GA:, :] = energy_ref[...]


def pick_kernel(base_ref, slots_ref, got_ref, out_ref, cond_ref):
    base = base_ref[0]
    row = lax.broadcasted_iota(jnp.int32, (SLOTS, GB), 0)
    for k in range(N_KA):
        energies = jnp.zeros((SLOTS, GB), f32)
        for s in range(SLOTS):
            local = slots_ref[k, s] - base
            mine = jnp.logical_and(local >= 0, local < N_PAIR)
            local = jnp.clip(local, 0, N_PAIR - 1)
            keep = jnp.where(mine, 1.0, 0.0).astype(f32)
            orbital = got_ref[local, OWN:OWN + GA, :].astype(f32)
            out_ref[k, s] = (orbital * keep).astype(bf16)
            level = got_ref[local, OWN + GA:, :].astype(f32)[:1] * keep
            energies = jnp.where(row == s, level, energies)
        out_ref[k, SLOTS] = energies.astype(bf16)
    for d in range(N_PAIR):
        cond_ref[d] = got_ref[d, :OWN, :]


def owner_kernel(count_ref, cond_ref, pick_ref, e_pick_ref, e_cond_ref, bd_ref, ta_ref, out_ref,
                 pair_s, first_s, moved_s, wtd_s, weight_s):
    live = lax.broadcasted_iota(jnp.int32, (SLOTS, BC), 0) < count_ref[0]
    weight_s[...] = jnp.where(live, 1.0, 0.0) * 2.0 / (e_cond_ref[...] - e_pick_ref[...])

    def to_first(i, carry):
        start = pl.multiple_of(i * 256, 256)
        cond = cond_ref[pl.ds(start, 256), :].astype(f32)
        pick = pick_ref[pl.ds(start, 256), :]
        for s in range(SLOTS):
            pair_s[:, s * BC:(s + 1) * BC] = (cond * pick[:, s:s + 1]).astype(bf16)
        first = jnp.dot(bd_ref[...], pair_s[...], preferred_element_type=f32).astype(bf16)
        for h in range(2):
            for kg in range(8):
                at = pl.multiple_of(kg * 256 + (2 * i + h) * 16, 16)
                first_s[pl.ds(at, 16), :] = first[h * 128 + kg * 16:h * 128 + kg * 16 + 16, :]
        return carry

    lax.fori_loop(0, 8, to_first, 0)

    def to_moved(kg, carry):
        start = pl.multiple_of(kg * 256, 256)
        moved = jnp.dot(ta_ref[...], first_s[pl.ds(start, 256), :], preferred_element_type=f32)
        moved = moved.astype(bf16)
        for j in range(GA):
            at = pl.multiple_of(j * GB + kg * 16, 16)
            rows = moved[j * 16:j * 16 + 16, :]
            moved_s[pl.ds(at, 16), :] = rows
            if j < WIN // GB:
                for s in range(SLOTS):
                    part = rows[:, s * BC:(s + 1) * BC].astype(f32) * weight_s[s:s + 1, :]
                    wtd_s[pl.ds(at, 16), s * BC:(s + 1) * BC] = part.astype(bf16)
        return carry

    lax.fori_loop(0, 8, to_moved, 0)

    def to_out(i, carry):
        start = pl.multiple_of(i * 256, 256)
        total = lax.dot_general(
            moved_s[pl.ds(start, 256), :], wtd_s[...], (((1,), (1,)), ((), ())),
            preferred_element_type=f32,
        )
        out_ref[pl.ds(start, 256), :] = (total * (2.0 / (SLOTS * BC * N_PAIR))).astype(bf16)
        return carry

    lax.fori_loop(0, 8, to_out, 0)


def shards(cond_orbitals, cond_energy, val_orbitals, val_energy, val_slots, owner_count):
    slots = lax.all_gather(val_slots[0], "ka", axis=0, tiled=True)
    base = (lax.axis_index("ka") * N_PAIR).astype(jnp.int32).reshape(1)

    packed = pl.pallas_call(
        pack_kernel,
        out_shape=jax.ShapeDtypeStruct((N_PAIR, BLOCK, BC), bf16),
        in_specs=vmem(3),
        out_specs=vmem(1)[0],
        compiler_params=params(),
        name="pack",
    )(cond_orbitals[0], val_orbitals.reshape(GA, GB), jnp.broadcast_to(val_energy[:, None], (8, GB)))
    got = lax.all_to_all(packed, "pair", 0, 0, tiled=True)

    routed, cond = pl.pallas_call(
        pick_kernel,
        out_shape=(
            jax.ShapeDtypeStruct((N_KA, SLOTS + 1, GA, GB), bf16),
            jax.ShapeDtypeStruct((N_PAIR, OWN, BC), bf16),
        ),
        in_specs=[pl.BlockSpec(memory_space=pltpu.SMEM)] * 2 + vmem(1),
        out_specs=tuple(vmem(2)),
        compiler_params=params(),
        name="pick",
    )(base, slots, got)
    routed = lax.all_to_all(routed, "ka", 0, 0, tiled=True)
    merged = jnp.sum(routed.astype(f32), axis=0)
    picked = merged[:SLOTS].reshape(SLOTS, GRID).T
    e_pick = merged[SLOTS]

    bd = jnp.kron(jnp.eye(2, dtype=f32), cosine_table(GB).astype(f32)).astype(bf16)
    ta = jnp.kron(cosine_table(GA).astype(f32), jnp.eye(16, dtype=f32)).astype(bf16)
    part = pl.pallas_call(
        owner_kernel,
        out_shape=jax.ShapeDtypeStruct((GRID, WIN), bf16),
        in_specs=[pl.BlockSpec(memory_space=pltpu.SMEM)] + vmem(6),
        out_specs=vmem(1)[0],
        scratch_shapes=[
            pltpu.VMEM((256, PAIRS), bf16),
            pltpu.VMEM((GRID, PAIRS), bf16),
            pltpu.VMEM((GRID, PAIRS), bf16),
            pltpu.VMEM((WIN, PAIRS), bf16),
            pltpu.VMEM((SLOTS, BC), f32),
        ],
        compiler_params=params(),
        name="owner",
    )(owner_count[0], cond.reshape(GRID, BC), picked, e_pick, cond_energy, bd, ta)

    parts = lax.all_to_all(part.reshape(N_PAIR, OWN, WIN), "pair", 0, 0, tiled=True)
    return jnp.sum(parts.astype(f32), axis=0)[None]


def solution(mesh):
    return jax.shard_map(
        shards,
        mesh=mesh,
        in_specs=(
            P("ka", "pair", None),
            P("ka", "pair"),
            P(("ka", "pair"), None),
            P(("ka", "pair")),
            P("ka", "pair", None),
            P("ka", "pair"),
        ),
        out_specs=P("ka", "pair", None),
        check_vma=False,
    )
```

time: 2330 us -> 159 us (0.07)
  the two profiles are of different devices: /device:TPU:2 before, /device:TPU:12 now
where the time goes in v1:
time: 159 us; the launch traced here: 158 us
  blocking collectives  87.4 us (55%)
  starting transfers between devices  23.4 us (15%)
  Pallas kernels  21.4 us (13%)
  waiting for transfers between devices  19.7 us (12%)
  other arithmetic  2.5 us (2%)
  local copies, waits for them, and re-layouts  2.41 us (2%)
    all_to_all x1, blocking collectives, shards(): lax.all_to_all(part.reshape(N_PAIR, OWN, WIN), 'pair', 0, 0, tiled=True)  65.6 us
    all_gather x1, blocking collectives, shards(): slots = lax.all_gather(val_slots[0], 'ka', axis=0, tiled=True)  21.8 us
    all_to_all x1, starting transfers between devices, shards(): got = lax.all_to_all(packed, 'pair', 0, 0, tiled=True)  19 us
    pallas_call x1, Pallas kernels, shards(): pl.pallas_call(owner_kernel, out_shape=jax.ShapeDtypeStruct((GRID, WIN),...  18.5 us
    all_to_all x1, waiting for transfers between devices, shards(): routed = lax.all_to_all(routed, 'ka', 0, 0, tiled=True)  13.9 us
    all_to_all x1, waiting for transfers between devices, shards(): got = lax.all_to_all(packed, 'pair', 0, 0, tiled=True)  5.86 us
    all_to_all x1, starting transfers between devices, shards(): routed = lax.all_to_all(routed, 'ka', 0, 0, tiled=True)  4.47 us
  transfers between devices with their start and end apart: 2, of which 2 were waited for; matrix products, arithmetic and copies ran while one was open for 1% of the time, Pallas kernels for 0%

profile of v1, /device:TPU:12, one launch (start us, length us, event | category | flops | bytes accessed | tf_op | source)
XLA Modules:
  0.0 158.4 jit_solution(16182536668316583115)
XLA Ops:
  0.0 0.0 copy-start.2
  0.7 0.7 reduce
  1.4 0.0 copy-start
  1.4 1.0 copy-done
  2.5 1.0 pack.1
  3.5 19.0 %all-to-all-start = ((bf16[64,56,128]{2,1,0:T(8,128)(2,1)}), bf16[64,56,128]{2,1,0:T(8,128)(2,1)S(1)}, u32[]{:S(2)}, u32[]{:S(2)}) async-start(bf16[64,56,128]{2,1,0:T(8,128)(2,1)} %pack.1), calls=%async_computation | async-start | bytes 1835008 | tf_op jit(solution)/shard_map/all_to_all | solution.py:126
  22.5 0.0 copy-done.2
  22.5 21.8 %all-gather = s32[8,1,16]{2,1,0:T(1,128)S(1)} all-gather(s32[1,1,16]{2,1,0:T(1,128)S(1)} %copy-done.2), channel_id=2, replica_groups=mesh['ka'=8,'pair'=64] {'ka'}, dimensions={0}, use_global_device_ids=true | all-gather | bytes 576 | tf_op jit(solution)/shard_map/all_gather | solution.py:115
  44.3 0.2 fusion
  44.6 5.9 %all-to-all-done.got_ref = bf16[64,56,128]{2,1,0:T(8,128)(2,1)S(1)} async-done(((bf16[64,56,128]{2,1,0:T(8,128)(2,1)}), bf16[64,56,128]{2,1,0:T(8,128)(2,1)S(1)}, u32[]{:S(2)}, u32[]{:S(2)}) %all-to-all-start) | async-done | bytes 917536 | tf_op jit(solution)/shard_map/all_to_all | solution.py:126
  50.5 1.9 %pick.1 = (bf16[8,17,16,128]{3,2,1,0:T(8,128)(2,1)}, bf16[64,32,128]{2,1,0:T(8,128)(2,1)S(1)}) custom-call(s32[1]{0:T(128)} %bitcast.1.base_ref, s32[8,16]{1,0:T(8,128)S(1)} %bitcast.29, bf16[64,56,128]{2,1,0:T(8,128)(2,1)S(1)} %all-to-all-done.got_ref), custom_call_target="tpu_custom_call" | custom-call | tf_op jit(solution)/shard_map/pick/pallas_call | solution.py:128
  52.3 4.5 %all-to-all-start.1 = ((bf16[8,17,16,128]{3,2,1,0:T(8,128)(2,1)}), bf16[8,17,16,128]{3,2,1,0:T(8,128)(2,1)S(1)}, u32[]{:S(2)}, u32[]{:S(2)}) async-start(bf16[8,17,16,128]{3,2,1,0:T(8,128)(2,1)} %get-tuple-element.8), calls=%async_computation.1 | async-start | bytes 1114112 | tf_op jit(solution)/shard_map/all_to_all | solution.py:139
  57.4 0.2 multiply_convert_fusion.1
  57.7 0.1 fusion.2
  57.7 0.0 copy-start.1
  57.7 0.2 multiply_convert_fusion
  58.0 1.0 convert_element_type.68.ta_ref
  59.0 13.9 %all-to-all-done.1 = bf16[8,17,16,128]{3,2,1,0:T(8,128)(2,1)S(1)} async-done(((bf16[8,17,16,128]{3,2,1,0:T(8,128)(2,1)}), bf16[8,17,16,128]{3,2,1,0:T(8,128)(2,1)S(1)}, u32[]{:S(2)}, u32[]{:S(2)}) %all-to-all-start.1) | async-done | bytes 557088 | tf_op jit(solution)/shard_map/all_to_all | solution.py:139
  72.8 0.1 convert_reduce_fusion.1
  72.9 0.3 copy.10
  73.3 0.0 copy-done.1
  73.3 18.5 %owner.1 = bf16[2048,512]{1,0:T(8,128)(2,1)S(1)} custom-call(s32[1]{0:T(128)} %bitcast.22.count_ref, bf16[2048,128]{1,0:T(8,128)(2,1)S(1)} %bitcast.25, f32[2048,16]{1,0:T(8,128)S(1)} %bitcast.24, f32[16,128]{1,0:T(8,128)S(1)} %slice_bitcast_fusion.e_pick_ref, f32[1,128]{1,0:T(1,128)S(1)} %copy-done.1, bf16[256,256]{1,0:T(8,128)(2,1)S(1)} %bitcast.26, ...), custom_call_target="tpu_custom_call" | custom-call | tf_op jit(solution)/shard_map/owner/pallas_call | solution.py:146
  91.8 65.6 %all_to_all.15 = bf16[64,32,512]{2,1,0:T(8,128)(2,1)S(1)} all-to-all(bf16[64,32,512]{2,1,0:T(8,128)(2,1)S(1)} %bitcast.23), channel_id=1, replica_groups=mesh['ka'=8,'pair'=64] {'pair'}, dimensions={0} | all-to-all | bytes 4194304 | tf_op jit(solution)/shard_map/all_to_all | solution.py:162
  157.4 1.0 convert_reduce_fusion
  (8 shorter events, 0.1 us)
Async XLA Ops:
  0.0 22.5 %copy-start.2 = (s32[1,1,16]{2,1,0:T(1,128)S(1)}, s32[1,1,16]{2,1,0:T(1,128)}, u32[]{:S(2)}) copy-start(s32[1,1,16]{2,1,0:T(1,128)} %param.10) | copy-start | bytes 196
  1.4 1.0 copy-start
  3.5 46.9 %all-to-all-start = ((bf16[64,56,128]{2,1,0:T(8,128)(2,1)}), bf16[64,56,128]{2,1,0:T(8,128)(2,1)S(1)}, u32[]{:S(2)}, u32[]{:S(2)}) async-start(bf16[64,56,128]{2,1,0:T(8,128)(2,1)} %pack.1), calls=%async_computation | async-start | bytes 1835008 | tf_op jit(solution)/shard_map/all_to_all | solution.py:126
  52.3 20.5 %all-to-all-start.1 = ((bf16[8,17,16,128]{3,2,1,0:T(8,128)(2,1)}), bf16[8,17,16,128]{3,2,1,0:T(8,128)(2,1)S(1)}, u32[]{:S(2)}, u32[]{:S(2)}) async-start(bf16[8,17,16,128]{3,2,1,0:T(8,128)(2,1)} %get-tuple-element.8), calls=%async_computation.1 | async-start | bytes 1114112 | tf_op jit(solution)/shard_map/all_to_all | solution.py:139
  57.7 15.6 %copy-start.1 = (f32[1,128]{1,0:T(1,128)S(1)}, f32[1,128]{1,0:T(1,128)}, u32[]{:S(2)}) copy-start(f32[1,128]{1,0:T(1,128)} %e_cond_ref.1) | copy-start | bytes 1540

commit v2 on v1

--- a/solution.py
+++ b/solution.py
@@ -3,7 +3,7 @@
 from jax import lax
 from jax.experimental import pallas as pl
 from jax.experimental.pallas import tpu as pltpu
-from jax.sharding import PartitionSpec as P
+from jax.sharding import Mesh, PartitionSpec as P
 
 BC = 128
 GA = 16
@@ -14,9 +14,15 @@
 NC = 8192
 N_KA = 8
 N_PAIR = 64
+N_Y = 8
+N_ZH = 2
+N_X = 4
 OWN = GRID // N_PAIR
+COLS_X = 384
 PAIRS = SLOTS * BC
 BLOCK = OWN + GA + 8
+
+PAIR = ("y", "zh", "x")
 
 f32 = jnp.float32
 bf16 = jnp.bfloat16
@@ -63,7 +69,7 @@
         cond_ref[d] = got_ref[d, :OWN, :]
 
 
-def owner_kernel(count_ref, cond_ref, pick_ref, e_pick_ref, e_cond_ref, bd_ref, ta_ref, out_ref,
+def owner_kernel(count_ref, cond_ref, pick_ref, e_pick_ref, e_cond_ref, bd_ref, ta_ref, x_ref, y_ref,
                  pair_s, first_s, moved_s, wtd_s, weight_s):
     live = lax.broadcasted_iota(jnp.int32, (SLOTS, BC), 0) < count_ref[0]
     weight_s[...] = jnp.where(live, 1.0, 0.0) * 2.0 / (e_cond_ref[...] - e_pick_ref[...])
@@ -105,7 +111,11 @@
             moved_s[pl.ds(start, 256), :], wtd_s[...], (((1,), (1,)), ((), ())),
             preferred_element_type=f32,
         )
-        out_ref[pl.ds(start, 256), :] = (total * (2.0 / (SLOTS * BC * N_PAIR))).astype(bf16)
+        total = (total * (2.0 / (SLOTS * BC * N_PAIR))).astype(bf16)
+        for t in range(8):
+            rows = total[t * OWN:(t + 1) * OWN]
+            x_ref[t % N_X, 2 * i + t // N_X] = rows[:, :COLS_X]
+            y_ref[i, t] = rows[:, COLS_X:]
         return carry
 
     lax.fori_loop(0, 8, to_out, 0)
@@ -123,7 +133,7 @@
         compiler_params=params(),
         name="pack",
     )(cond_orbitals[0], val_orbitals.reshape(GA, GB), jnp.broadcast_to(val_energy[:, None], (8, GB)))
-    got = lax.all_to_all(packed, "pair", 0, 0, tiled=True)
+    got = lax.all_to_all(packed, PAIR, 0, 0, tiled=True)
 
     routed, cond = pl.pallas_call(
         pick_kernel,
@@ -143,11 +153,14 @@
 
     bd = jnp.kron(jnp.eye(2, dtype=f32), cosine_table(GB).astype(f32)).astype(bf16)
     ta = jnp.kron(cosine_table(GA).astype(f32), jnp.eye(16, dtype=f32)).astype(bf16)
-    part = pl.pallas_call(
+    part_x, part_y = pl.pallas_call(
         owner_kernel,
-        out_shape=jax.ShapeDtypeStruct((GRID, WIN), bf16),
+        out_shape=(
+            jax.ShapeDtypeStruct((N_X, N_Y * N_ZH, OWN, COLS_X), bf16),
+            jax.ShapeDtypeStruct((N_Y, N_ZH * N_X, OWN, WIN - COLS_X), bf16),
+        ),
         in_specs=[pl.BlockSpec(memory_space=pltpu.SMEM)] + vmem(6),
-        out_specs=vmem(1)[0],
+        out_specs=tuple(vmem(2)),
         scratch_shapes=[
             pltpu.VMEM((256, PAIRS), bf16),
             pltpu.VMEM((GRID, PAIRS), bf16),
@@ -159,22 +172,30 @@
         name="owner",
     )(owner_count[0], cond.reshape(GRID, BC), picked, e_pick, cond_energy, bd, ta)
 
-    parts = lax.all_to_all(part.reshape(N_PAIR, OWN, WIN), "pair", 0, 0, tiled=True)
-    return jnp.sum(parts.astype(f32), axis=0)[None]
+    part_x = lax.all_to_all(part_x, "x", 0, 0, tiled=True)
+    part_y = lax.all_to_all(part_y, "y", 0, 0, tiled=True)
+    part_x = jnp.sum(part_x.astype(f32), axis=0).astype(bf16)
+    part_y = jnp.sum(part_y.astype(f32), axis=0).astype(bf16)
+    part_x = lax.all_to_all(part_x, ("y", "zh"), 0, 0, tiled=True)
+    part_y = lax.all_to_all(part_y, ("zh", "x"), 0, 0, tiled=True)
+    part_x = jnp.sum(part_x.astype(f32), axis=0)
+    part_y = jnp.sum(part_y.astype(f32), axis=0)
+    return jnp.concatenate([part_x, part_y], axis=1)[None]
 
 
 def solution(mesh):
+    mesh = Mesh(mesh.devices.reshape(N_KA, N_Y, N_ZH, N_X), ("ka", "y", "zh", "x"))
     return jax.shard_map(
         shards,
         mesh=mesh,
         in_specs=(
-            P("ka", "pair", None),
-            P("ka", "pair"),
-            P(("ka", "pair"), None),
-            P(("ka", "pair")),
-            P("ka", "pair", None),
-            P("ka", "pair"),
+            P("ka", PAIR, None),
+            P("ka", PAIR),
+            P(("ka",) + PAIR, None),
+            P(("ka",) + PAIR),
+            P("ka", PAIR, None),
+            P("ka", PAIR),
         ),
-        out_specs=P("ka", "pair", None),
+        out_specs=P("ka", PAIR, None),
         check_vma=False,
     )

time: 159 us -> 174 us (1.094)
  the two profiles are of different devices: /device:TPU:12 before, /device:TPU:2 now
where the time goes in v2:
time: 174 us
  waiting for transfers between devices  61.3 us (35%)
  blocking collectives  42.4 us (24%)
  starting transfers between devices  39.5 us (23%)
  Pallas kernels  22.6 us (13%)
  other arithmetic  4.02 us (2%)
  local copies, waits for them, and re-layouts  2.41 us (1%)
    all_to_all x1, blocking collectives, shards(): part_y = lax.all_to_all(part_y, 'y', 0, 0, tiled=True)  21.5 us
    all_gather x1, blocking collectives, shards(): slots = lax.all_gather(val_slots[0], 'ka', axis=0, tiled=True)  20.9 us
    pallas_call x1, Pallas kernels, shards(): pl.pallas_call(owner_kernel, out_shape=(jax.ShapeDtypeStruct((N_X, N_Y *...  19.7 us
    all_to_all x1, starting transfers between devices, shards(): got = lax.all_to_all(packed, PAIR, 0, 0, tiled=True)  19.1 us
    all_to_all x1, waiting for transfers between devices, shards(): part_x = lax.all_to_all(part_x, 'x', 0, 0, tiled=True)  16.8 us
    all_to_all x1, waiting for transfers between devices, shards(): part_x = lax.all_to_all(part_x, ('y', 'zh'), 0, 0, tiled=True)  15.8 us
    all_to_all x1, waiting for transfers between devices, shards(): routed = lax.all_to_all(routed, 'ka', 0, 0, tiled=True)  13.9 us
    all_to_all x1, waiting for transfers between devices, shards(): part_y = lax.all_to_all(part_y, ('zh', 'x'), 0, 0, tiled=True)  7.73 us
  transfers between devices with their start and end apart: 5, of which 5 were waited for; matrix products, arithmetic and copies ran while one was open for 2% of the time, Pallas kernels for 0%

profile of v2, /device:TPU:2, one launch (start us, length us, event | category | flops | bytes accessed | tf_op | source)
XLA Modules:
  0.0 173.7 jit_solution(1841060833540819106)
XLA Ops:
  0.7 0.7 reduce.2
  1.4 0.0 copy-start
  1.4 1.0 copy-done
  2.4 0.0 copy-start.2
  2.4 1.1 pack.1
  3.5 19.1 %all-to-all-start = ((bf16[64,56,128]{2,1,0:T(8,128)(2,1)}), bf16[64,56,128]{2,1,0:T(8,128)(2,1)S(1)}, u32[]{:S(2)}, u32[]{:S(2)}) async-start(bf16[64,56,128]{2,1,0:T(8,128)(2,1)} %pack.1), calls=%async_computation | async-start | bytes 1835008 | tf_op jit(solution)/shard_map/all_to_all | solution.py:136
  22.6 0.0 copy-done.2
  22.6 20.9 %all-gather = s32[8,1,16]{2,1,0:T(1,128)S(1)} all-gather(s32[1,1,16]{2,1,0:T(1,128)S(1)} %copy-done.2), channel_id=2, replica_groups=mesh['ka'=8,'y'=8,'zh'=2,'x'=4] {'ka'}, dimensions={0}, use_global_device_ids=true | all-gather | bytes 576 | tf_op jit(solution)/shard_map/all_gather | solution.py:125
  43.5 0.2 fusion
  43.8 7.1 %all-to-all-done.got_ref = bf16[64,56,128]{2,1,0:T(8,128)(2,1)S(1)} async-done(((bf16[64,56,128]{2,1,0:T(8,128)(2,1)}), bf16[64,56,128]{2,1,0:T(8,128)(2,1)S(1)}, u32[]{:S(2)}, u32[]{:S(2)}) %all-to-all-start) | async-done | bytes 917536 | tf_op jit(solution)/shard_map/all_to_all | solution.py:136
  50.9 1.9 %pick.1 = (bf16[8,17,16,128]{3,2,1,0:T(8,128)(2,1)}, bf16[64,32,128]{2,1,0:T(8,128)(2,1)S(1)}) custom-call(s32[1]{0:T(128)} %bitcast.1.base_ref, s32[8,16]{1,0:T(8,128)S(1)} %bitcast.28, bf16[64,56,128]{2,1,0:T(8,128)(2,1)S(1)} %all-to-all-done.got_ref), custom_call_target="tpu_custom_call" | custom-call | tf_op jit(solution)/shard_map/pick/pallas_call | solution.py:138
  52.7 4.5 %all-to-all-start.1 = ((bf16[8,17,16,128]{3,2,1,0:T(8,128)(2,1)}), bf16[8,17,16,128]{3,2,1,0:T(8,128)(2,1)S(1)}, u32[]{:S(2)}, u32[]{:S(2)}) async-start(bf16[8,17,16,128]{3,2,1,0:T(8,128)(2,1)} %get-tuple-element.10), calls=%async_computation.1 | async-start | bytes 1114112 | tf_op jit(solution)/shard_map/all_to_all | solution.py:149
  57.9 0.2 multiply_convert_fusion.1
  58.1 0.1 fusion.2
  58.2 0.2 multiply_convert_fusion
  58.4 0.0 copy-start.1
  58.4 1.0 convert_element_type.75.ta_ref
  59.4 13.9 %all-to-all-done.1 = bf16[8,17,16,128]{3,2,1,0:T(8,128)(2,1)S(1)} async-done(((bf16[8,17,16,128]{3,2,1,0:T(8,128)(2,1)}), bf16[8,17,16,128]{3,2,1,0:T(8,128)(2,1)S(1)}, u32[]{:S(2)}, u32[]{:S(2)}) %all-to-all-start.1) | async-done | bytes 557088 | tf_op jit(solution)/shard_map/all_to_all | solution.py:149
  73.3 0.1 convert_reduce_fusion
  73.4 0.3 copy.11
  73.7 0.0 copy-done.1
  73.7 19.7 %owner.1 = (bf16[4,16,32,384]{3,2,1,0:T(8,128)(2,1)}, bf16[8,8,32,128]{3,2,1,0:T(8,128)(2,1)S(1)}) custom-call(s32[1]{0:T(128)} %bitcast.22.count_ref, bf16[2048,128]{1,0:T(8,128)(2,1)S(1)} %bitcast.24, f32[2048,16]{1,0:T(8,128)S(1)} %bitcast.23, f32[16,128]{1,0:T(8,128)S(1)} %slice_bitcast_fusion.e_pick_ref, f32[1,128]{1,0:T(1,128)S(1)} %copy-done.1, ...), custom_call_target="tpu_custom_call" | custom-call | tf_op jit(solution)/shard_map/owner/pallas_call | solution.py:156
  93.4 21.5 %all_to_all.30 = bf16[8,8,32,128]{3,2,1,0:T(8,128)(2,1)S(1)} all-to-all(bf16[8,8,32,128]{3,2,1,0:T(8,128)(2,1)S(1)} %get-tuple-element.12), channel_id=1, replica_groups=mesh['ka'=8,'y'=8,'zh'=2,'x'=4] {'y'}, dimensions={0} | all-to-all | bytes 1048576 | tf_op jit(solution)/shard_map/all_to_all | solution.py:176
  114.9 4.9 %all-to-all-start.2 = ((bf16[4,16,32,384]{3,2,1,0:T(8,128)(2,1)}), bf16[4,16,32,384]{3,2,1,0:T(8,128)(2,1)S(1)}, u32[]{:S(2)}, u32[]{:S(2)}) async-start(bf16[4,16,32,384]{3,2,1,0:T(8,128)(2,1)} %get-tuple-element.11), calls=%async_computation.2 | async-start | bytes 3145728 | tf_op jit(solution)/shard_map/all_to_all | solution.py:175
  119.8 0.7 reduce_sum.54
  120.5 16.8 %all-to-all-done.2 = bf16[4,16,32,384]{3,2,1,0:T(8,128)(2,1)S(1)} async-done(((bf16[4,16,32,384]{3,2,1,0:T(8,128)(2,1)}), bf16[4,16,32,384]{3,2,1,0:T(8,128)(2,1)S(1)}, u32[]{:S(2)}, u32[]{:S(2)}) %all-to-all-start.2) | async-done | bytes 1572896 | tf_op jit(solution)/shard_map/all_to_all | solution.py:175
  137.3 7.5 %all-to-all-start.5 = ((bf16[8,32,128]{2,1,0:T(8,128)(2,1)}), bf16[8,32,128]{2,1,0:T(8,128)(2,1)S(1)}, u32[]{:S(2)}, u32[]{:S(2)}) async-start(bf16[8,32,128]{2,1,0:T(8,128)(2,1)} %reduce_sum.54), calls=%async_computation.5 | async-start | bytes 131072 | tf_op jit(solution)/shard_map/all_to_all | solution.py:180
  144.8 1.1 reduce_sum.52
  145.9 7.7 %all-to-all-done.5 = bf16[8,32,128]{2,1,0:T(8,128)(2,1)S(1)} async-done(((bf16[8,32,128]{2,1,0:T(8,128)(2,1)}), bf16[8,32,128]{2,1,0:T(8,128)(2,1)S(1)}, u32[]{:S(2)}, u32[]{:S(2)}) %all-to-all-start.5) | async-done | bytes 65568 | tf_op jit(solution)/shard_map/all_to_all | solution.py:180
  153.6 3.6 %all-to-all-start.3 = ((bf16[16,32,384]{2,1,0:T(8,128)(2,1)}), bf16[16,32,384]{2,1,0:T(8,128)(2,1)S(1)}, u32[]{:S(2)}, u32[]{:S(2)}) async-start(bf16[16,32,384]{2,1,0:T(8,128)(2,1)} %reduce_sum.52), calls=%async_computation.3 | async-start | bytes 786432 | tf_op jit(solution)/shard_map/all_to_all | solution.py:179
  157.2 15.8 %all-to-all-done.3 = bf16[16,32,384]{2,1,0:T(8,128)(2,1)S(1)} async-done(((bf16[16,32,384]{2,1,0:T(8,128)(2,1)}), bf16[16,32,384]{2,1,0:T(8,128)(2,1)S(1)}, u32[]{:S(2)}, u32[]{:S(2)}) %all-to-all-start.3) | async-done | bytes 393248 | tf_op jit(solution)/shard_map/all_to_all | solution.py:179
  173.0 0.1 convert_reduce_fusion.1
  173.0 0.6 maximum_bitcast_fusion
  (9 shorter events, 0.1 us)
Async XLA Ops:
  1.4 1.0 copy-start
  2.4 20.2 %copy-start.2 = (s32[1,1,16]{2,1,0:T(1,128)S(1)}, s32[1,1,16]{2,1,0:T(1,128)}, u32[]{:S(2)}) copy-start(s32[1,1,16]{2,1,0:T(1,128)} %param.10) | copy-start | bytes 196
  3.5 47.4 %all-to-all-start = ((bf16[64,56,128]{2,1,0:T(8,128)(2,1)}), bf16[64,56,128]{2,1,0:T(8,128)(2,1)S(1)}, u32[]{:S(2)}, u32[]{:S(2)}) async-start(bf16[64,56,128]{2,1,0:T(8,128)(2,1)} %pack.1), calls=%async_computation | async-start | bytes 1835008 | tf_op jit(solution)/shard_map/all_to_all | solution.py:136
  52.7 20.6 %all-to-all-start.1 = ((bf16[8,17,16,128]{3,2,1,0:T(8,128)(2,1)}), bf16[8,17,16,128]{3,2,1,0:T(8,128)(2,1)S(1)}, u32[]{:S(2)}, u32[]{:S(2)}) async-start(bf16[8,17,16,128]{3,2,1,0:T(8,128)(2,1)} %get-tuple-element.10), calls=%async_computation.1 | async-start | bytes 1114112 | tf_op jit(solution)/shard_map/all_to_all | solution.py:149
  58.4 15.3 %copy-start.1 = (f32[1,128]{1,0:T(1,128)S(1)}, f32[1,128]{1,0:T(1,128)}, u32[]{:S(2)}) copy-start(f32[1,128]{1,0:T(1,128)} %e_cond_ref.1) | copy-start | bytes 1540
  114.9 22.4 %all-to-all-start.2 = ((bf16[4,16,32,384]{3,2,1,0:T(8,128)(2,1)}), bf16[4,16,32,384]{3,2,1,0:T(8,128)(2,1)S(1)}, u32[]{:S(2)}, u32[]{:S(2)}) async-start(bf16[4,16,32,384]{3,2,1,0:T(8,128)(2,1)} %get-tuple-element.11), calls=%async_computation.2 | async-start | bytes 3145728 | tf_op jit(solution)/shard_map/all_to_all | solution.py:175
  137.3 16.3 %all-to-all-start.5 = ((bf16[8,32,128]{2,1,0:T(8,128)(2,1)}), bf16[8,32,128]{2,1,0:T(8,128)(2,1)S(1)}, u32[]{:S(2)}, u32[]{:S(2)}) async-start(bf16[8,32,128]{2,1,0:T(8,128)(2,1)} %reduce_sum.54), calls=%async_computation.5 | async-start | bytes 131072 | tf_op jit(solution)/shard_map/all_to_all | solution.py:180
  153.6 19.4 %all-to-all-start.3 = ((bf16[16,32,384]{2,1,0:T(8,128)(2,1)}), bf16[16,32,384]{2,1,0:T(8,128)(2,1)S(1)}, u32[]{:S(2)}, u32[]{:S(2)}) async-start(bf16[16,32,384]{2,1,0:T(8,128)(2,1)} %reduce_sum.52), calls=%async_computation.3 | async-start | bytes 786432 | tf_op jit(solution)/shard_map/all_to_all | solution.py:179

commit v3 on v2

--- a/solution.py
+++ b/solution.py
@@ -18,7 +18,6 @@
 N_ZH = 2
 N_X = 4
 OWN = GRID // N_PAIR
-COLS_X = 384
 PAIRS = SLOTS * BC
 BLOCK = OWN + GA + 8
 
@@ -69,7 +68,7 @@
         cond_ref[d] = got_ref[d, :OWN, :]
 
 
-def owner_kernel(count_ref, cond_ref, pick_ref, e_pick_ref, e_cond_ref, bd_ref, ta_ref, x_ref, y_ref,
+def owner_kernel(count_ref, cond_ref, pick_ref, e_pick_ref, e_cond_ref, bd_ref, ta_ref, out_ref,
                  pair_s, first_s, moved_s, wtd_s, weight_s):
     live = lax.broadcasted_iota(jnp.int32, (SLOTS, BC), 0) < count_ref[0]
     weight_s[...] = jnp.where(live, 1.0, 0.0) * 2.0 / (e_cond_ref[...] - e_pick_ref[...])
@@ -113,9 +112,7 @@
         )
         total = (total * (2.0 / (SLOTS * BC * N_PAIR))).astype(bf16)
         for t in range(8):
-            rows = total[t * OWN:(t + 1) * OWN]
-            x_ref[t % N_X, 2 * i + t // N_X] = rows[:, :COLS_X]
-            y_ref[i, t] = rows[:, COLS_X:]
+            out_ref[t % N_X, 2 * i + t // N_X] = total[t * OWN:(t + 1) * OWN]
         return carry
 
     lax.fori_loop(0, 8, to_out, 0)
@@ -153,14 +150,11 @@
 
     bd = jnp.kron(jnp.eye(2, dtype=f32), cosine_table(GB).astype(f32)).astype(bf16)
     ta = jnp.kron(cosine_table(GA).astype(f32), jnp.eye(16, dtype=f32)).astype(bf16)
-    part_x, part_y = pl.pallas_call(
+    part = pl.pallas_call(
         owner_kernel,
-        out_shape=(
-            jax.ShapeDtypeStruct((N_X, N_Y * N_ZH, OWN, COLS_X), bf16),
-            jax.ShapeDtypeStruct((N_Y, N_ZH * N_X, OWN, WIN - COLS_X), bf16),
-        ),
+        out_shape=jax.ShapeDtypeStruct((N_X, N_Y * N_ZH, OWN, WIN), bf16),
         in_specs=[pl.BlockSpec(memory_space=pltpu.SMEM)] + vmem(6),
-        out_specs=tuple(vmem(2)),
+        out_specs=vmem(1)[0],
         scratch_shapes=[
             pltpu.VMEM((256, PAIRS), bf16),
             pltpu.VMEM((GRID, PAIRS), bf16),
@@ -172,15 +166,10 @@
         name="owner",
     )(owner_count[0], cond.reshape(GRID, BC), picked, e_pick, cond_energy, bd, ta)
 
-    part_x = lax.all_to_all(part_x, "x", 0, 0, tiled=True)
-    part_y = lax.all_to_all(part_y, "y", 0, 0, tiled=True)
-    part_x = jnp.sum(part_x.astype(f32), axis=0).astype(bf16)
-    part_y = jnp.sum(part_y.astype(f32), axis=0).astype(bf16)
-    part_x = lax.all_to_all(part_x, ("y", "zh"), 0, 0, tiled=True)
-    part_y = lax.all_to_all(part_y, ("zh", "x"), 0, 0, tiled=True)
-    part_x = jnp.sum(part_x.astype(f32), axis=0)
-    part_y = jnp.sum(part_y.astype(f32), axis=0)
-    return jnp.concatenate([part_x, part_y], axis=1)[None]
+    part = lax.all_to_all(part, "x", 0, 0, tiled=True)
+    part = jnp.sum(part.astype(f32), axis=0).astype(bf16)
+    part = lax.all_to_all(part, ("y", "zh"), 0, 0, tiled=True)
+    return jnp.sum(part.astype(f32), axis=0)[None]
 
 
 def solution(mesh):

time: 174 us -> 151 us (0.87)
  the two profiles are of different devices: /device:TPU:2 before, /device:TPU:16 now
where the time goes in v3:
time: 151 us; the launch traced here: 150 us
  blocking collectives  78.5 us (52%)
  starting transfers between devices  23.4 us (15%)
  Pallas kernels  21.4 us (14%)
  waiting for transfers between devices  20.4 us (14%)
  other arithmetic  2.67 us (2%)
  local copies, waits for them, and re-layouts  2.41 us (2%)
    all_to_all x1, blocking collectives, shards(): part = lax.all_to_all(part, 'x', 0, 0, tiled=True)  30.2 us
    all_to_all x1, blocking collectives, shards(): part = lax.all_to_all(part, ('y', 'zh'), 0, 0, tiled=True)  27.4 us
    all_gather x1, blocking collectives, shards(): slots = lax.all_gather(val_slots[0], 'ka', axis=0, tiled=True)  20.9 us
    all_to_all x1, starting transfers between devices, shards(): got = lax.all_to_all(packed, PAIR, 0, 0, tiled=True)  18.9 us
    pallas_call x1, Pallas kernels, shards(): pl.pallas_call(owner_kernel, out_shape=jax.ShapeDtypeStruct((N_X, N_Y * N...  18.5 us
    all_to_all x1, waiting for transfers between devices, shards(): routed = lax.all_to_all(routed, 'ka', 0, 0, tiled=True)  13.9 us
    all_to_all x1, waiting for transfers between devices, shards(): got = lax.all_to_all(packed, PAIR, 0, 0, tiled=True)  6.53 us
    all_to_all x1, starting transfers between devices, shards(): routed = lax.all_to_all(routed, 'ka', 0, 0, tiled=True)  4.55 us
  transfers between devices with their start and end apart: 2, of which 2 were waited for; matrix products, arithmetic and copies ran while one was open for 1% of the time, Pallas kernels for 0%

profile of v3, /device:TPU:16, one launch (start us, length us, event | category | flops | bytes accessed | tf_op | source)
XLA Modules:
  0.0 150.3 jit_solution(9841631446896569937)
XLA Ops:
  0.0 0.0 copy-start.2
  0.7 0.7 reduce.1
  1.4 0.0 copy-start
  1.4 1.0 copy-done
  2.5 1.1 pack.1
  3.5 18.9 %all-to-all-start = ((bf16[64,56,128]{2,1,0:T(8,128)(2,1)}), bf16[64,56,128]{2,1,0:T(8,128)(2,1)S(1)}, u32[]{:S(2)}, u32[]{:S(2)}) async-start(bf16[64,56,128]{2,1,0:T(8,128)(2,1)} %pack.1), calls=%async_computation | async-start | bytes 1835008 | tf_op jit(solution)/shard_map/all_to_all | solution.py:133
  22.4 0.0 copy-done.2
  22.4 20.9 %all-gather = s32[8,1,16]{2,1,0:T(1,128)S(1)} all-gather(s32[1,1,16]{2,1,0:T(1,128)S(1)} %copy-done.2), channel_id=2, replica_groups=mesh['ka'=8,'y'=8,'zh'=2,'x'=4] {'ka'}, dimensions={0}, use_global_device_ids=true | all-gather | bytes 576 | tf_op jit(solution)/shard_map/all_gather | solution.py:122
  43.4 0.2 fusion
  43.6 6.5 %all-to-all-done.got_ref = bf16[64,56,128]{2,1,0:T(8,128)(2,1)S(1)} async-done(((bf16[64,56,128]{2,1,0:T(8,128)(2,1)}), bf16[64,56,128]{2,1,0:T(8,128)(2,1)S(1)}, u32[]{:S(2)}, u32[]{:S(2)}) %all-to-all-start) | async-done | bytes 917536 | tf_op jit(solution)/shard_map/all_to_all | solution.py:133
  50.2 1.9 %pick.1 = (bf16[8,17,16,128]{3,2,1,0:T(8,128)(2,1)}, bf16[64,32,128]{2,1,0:T(8,128)(2,1)S(1)}) custom-call(s32[1]{0:T(128)} %bitcast.1.base_ref, s32[8,16]{1,0:T(8,128)S(1)} %bitcast.27, bf16[64,56,128]{2,1,0:T(8,128)(2,1)S(1)} %all-to-all-done.got_ref), custom_call_target="tpu_custom_call" | custom-call | tf_op jit(solution)/shard_map/pick/pallas_call | solution.py:135
  52.0 4.5 %all-to-all-start.1 = ((bf16[8,17,16,128]{3,2,1,0:T(8,128)(2,1)}), bf16[8,17,16,128]{3,2,1,0:T(8,128)(2,1)S(1)}, u32[]{:S(2)}, u32[]{:S(2)}) async-start(bf16[8,17,16,128]{3,2,1,0:T(8,128)(2,1)} %get-tuple-element.8), calls=%async_computation.1 | async-start | bytes 1114112 | tf_op jit(solution)/shard_map/all_to_all | solution.py:146
  57.2 0.2 multiply_convert_fusion.1
  57.4 0.1 fusion.2
  57.5 0.0 copy-start.1
  57.5 0.2 multiply_convert_fusion
  57.8 1.0 convert_element_type.70.ta_ref
  58.7 13.9 %all-to-all-done.1 = bf16[8,17,16,128]{3,2,1,0:T(8,128)(2,1)S(1)} async-done(((bf16[8,17,16,128]{3,2,1,0:T(8,128)(2,1)}), bf16[8,17,16,128]{3,2,1,0:T(8,128)(2,1)S(1)}, u32[]{:S(2)}, u32[]{:S(2)}) %all-to-all-start.1) | async-done | bytes 557088 | tf_op jit(solution)/shard_map/all_to_all | solution.py:146
  72.6 0.1 convert_reduce_fusion
  72.7 0.3 copy.11
  73.1 0.0 copy-done.1
  73.1 18.5 %owner.1 = bf16[4,16,32,512]{3,2,1,0:T(8,128)(2,1)S(1)} custom-call(s32[1]{0:T(128)} %bitcast.21.count_ref, bf16[2048,128]{1,0:T(8,128)(2,1)S(1)} %bitcast.23, f32[2048,16]{1,0:T(8,128)S(1)} %bitcast.22, f32[16,128]{1,0:T(8,128)S(1)} %slice_bitcast_fusion.e_pick_ref, f32[1,128]{1,0:T(1,128)S(1)} %copy-done.1, bf16[256,256]{1,0:T(8,128)(2,1)S(1)} %bitcast.24, ...), custom_call_target="tpu_custom_call" | custom-call | tf_op jit(solution)/shard_map/owner/pallas_call | solution.py:153
  91.6 30.2 %all_to_all.20 = bf16[4,16,32,512]{3,2,1,0:T(8,128)(2,1)S(1)} all-to-all(bf16[4,16,32,512]{3,2,1,0:T(8,128)(2,1)S(1)} %owner.1), channel_id=1, replica_groups=mesh['ka'=8,'y'=8,'zh'=2,'x'=4] {'x'}, dimensions={0} | all-to-all | bytes 4194304 | tf_op jit(solution)/shard_map/all_to_all | solution.py:169
  121.8 0.4 reduce_sum.31
  122.2 27.4 %all_to_all.21 = bf16[16,32,512]{2,1,0:T(8,128)(2,1)S(1)} all-to-all(bf16[16,32,512]{2,1,0:T(8,128)(2,1)S(1)} %reduce_sum.31), channel_id=1, replica_groups=mesh['ka'=8,'y'=8,'zh'=2,'x'=4] {'y','zh'}, dimensions={0} | all-to-all | bytes 1048576 | tf_op jit(solution)/shard_map/all_to_all | solution.py:171
  149.6 0.7 convert_reduce_fusion.1
  (8 shorter events, 0.1 us)
Async XLA Ops:
  0.0 22.4 %copy-start.2 = (s32[1,1,16]{2,1,0:T(1,128)S(1)}, s32[1,1,16]{2,1,0:T(1,128)}, u32[]{:S(2)}) copy-start(s32[1,1,16]{2,1,0:T(1,128)} %param.10) | copy-start | bytes 196
  1.4 1.0 copy-start
  3.5 46.7 %all-to-all-start = ((bf16[64,56,128]{2,1,0:T(8,128)(2,1)}), bf16[64,56,128]{2,1,0:T(8,128)(2,1)S(1)}, u32[]{:S(2)}, u32[]{:S(2)}) async-start(bf16[64,56,128]{2,1,0:T(8,128)(2,1)} %pack.1), calls=%async_computation | async-start | bytes 1835008 | tf_op jit(solution)/shard_map/all_to_all | solution.py:133
  52.0 20.6 %all-to-all-start.1 = ((bf16[8,17,16,128]{3,2,1,0:T(8,128)(2,1)}), bf16[8,17,16,128]{3,2,1,0:T(8,128)(2,1)S(1)}, u32[]{:S(2)}, u32[]{:S(2)}) async-start(bf16[8,17,16,128]{3,2,1,0:T(8,128)(2,1)} %get-tuple-element.8), calls=%async_computation.1 | async-start | bytes 1114112 | tf_op jit(solution)/shard_map/all_to_all | solution.py:146
  57.5 15.6 %copy-start.1 = (f32[1,128]{1,0:T(1,128)S(1)}, f32[1,128]{1,0:T(1,128)}, u32[]{:S(2)}) copy-start(f32[1,128]{1,0:T(1,128)} %e_cond_ref.1) | copy-start | bytes 1540

commit v4 on v3

v4 whole, which is shorter than its diff:
```python
import jax
import jax.numpy as jnp
from jax import lax
from jax.experimental import pallas as pl
from jax.experimental.pallas import tpu as pltpu
from jax.sharding import Mesh, PartitionSpec as P

BC = 128
GA = 16
GB = 128
WIN = 512
SLOTS = 16
GRID = 2048
NC = 8192
N_KA = 8
N_PAIR = 64
N_Y = 8
N_ZH = 2
N_X = 4
OWN = GRID // N_PAIR
PAIRS = SLOTS * BC
GROUP = 4
BLOCK = OWN + 2 * N_KA + N_KA
ENERGY = OWN + 2 * N_KA

PAIR = ("y", "zh", "x")

f32 = jnp.float32
bf16 = jnp.bfloat16


def cosine_table(length):
    freq = lax.iota(jnp.float32, length)[:, None]
    point = lax.iota(jnp.float32, length)[None, :]
    factor = jnp.where(freq == 0, jnp.sqrt(1.0 / length), jnp.sqrt(2.0 / length))
    return (factor * jnp.cos(jnp.pi * (point + 0.5) * freq / length)).astype(jnp.bfloat16)


def vmem(count):
    return [pl.BlockSpec(memory_space=pltpu.VMEM)] * count


def params():
    return pltpu.CompilerParams(vmem_limit_bytes=48 * 2**20)


def pack_kernel(cond_ref, pieces_ref, out_ref):
    points = jnp.concatenate([pieces_ref[k, :2, :] for k in range(N_KA)], axis=0).astype(bf16)
    levels = jnp.concatenate([pieces_ref[k, 2:3, :] for k in range(N_KA)], axis=0).astype(bf16)
    for d in range(N_PAIR):
        out_ref[d, :OWN, :] = cond_ref[:, d * BC:(d + 1) * BC]
        out_ref[d, OWN:ENERGY, :] = points
        out_ref[d, ENERGY:, :] = levels


def pick_kernel(slots_ref, got_ref, out_ref, rows_s, picked_s):
    for d in range(N_PAIR):
        rows_s[d] = got_ref[d, OWN:, :].astype(f32)
    for k in range(N_KA):
        for s in range(SLOTS):
            slot = slots_ref[k, s]
            owner = lax.rem(slot, N_PAIR)
            line = lax.div(slot, N_PAIR)
            for a in range(2):
                picked_s[k, a, s:s + 1, :] = rows_s[owner, pl.ds(2 * line + a, 1), :]
            picked_s[k, 2, s:s + 1, :] = rows_s[owner, pl.ds(2 * N_KA + line, 1), :]
    out_ref[...] = picked_s[...].astype(bf16)


def owner_kernel(count_ref, got_ref, pick_ref, e_cond_ref, bd_ref, ta_ref, out_ref,
                 first_s, moved_s, wtd_s, weight_s):
    live = lax.broadcasted_iota(jnp.int32, (SLOTS, BC), 0) < count_ref[0]
    e_pick = pick_ref[0, 2].astype(f32)
    weight_s[...] = jnp.where(live, 1.0, 0.0) * 2.0 / (e_cond_ref[...] - e_pick)

    def to_first(i, carry):
        cond = [got_ref[8 * i + t, :OWN, :].astype(f32) for t in range(8)]
        cond = [jnp.concatenate(cond[4 * h:4 * h + 4], axis=0) for h in range(2)]
        pick = [pick_ref[i, h].astype(f32).T for h in range(2)]
        for s0 in range(0, SLOTS, GROUP):
            pair = [
                jnp.concatenate([cond[h] * pick[h][:, s:s + 1] for h in range(2)], axis=0).astype(bf16)
                for s in range(s0, s0 + GROUP)
            ]
            pair = jnp.concatenate(pair, axis=1)
            first = jnp.dot(bd_ref[...], pair, preferred_element_type=f32).astype(bf16)
            for h in range(2):
                for kg in range(8):
                    at = pl.multiple_of(kg * 256 + (2 * i + h) * 16, 16)
                    row = h * GB + kg * 16
                    first_s[pl.ds(at, 16), s0 * BC:(s0 + GROUP) * BC] = first[row:row + 16, :]
        return carry

    lax.fori_loop(0, 8, to_first, 0, unroll=4)

    def to_moved(kg, carry):
        start = pl.multiple_of(kg * 256, 256)
        for s0 in range(0, SLOTS, GROUP):
            lanes = slice(s0 * BC, (s0 + GROUP) * BC)
            moved = jnp.dot(ta_ref[...], first_s[pl.ds(start, 256), lanes], preferred_element_type=f32)
            moved = moved.astype(bf16)
            for j in range(GA):
                at = pl.multiple_of(j * GB + kg * 16, 16)
                rows = moved[j * 16:j * 16 + 16, :]
                moved_s[pl.ds(at, 16), lanes] = rows
                if j < WIN // GB:
                    for t in range(GROUP):
                        s = s0 + t
                        part = rows[:, t * BC:(t + 1) * BC].astype(f32) * weight_s[s:s + 1, :]
                        wtd_s[pl.ds(at, 16), s * BC:(s + 1) * BC] = part.astype(bf16)
        return carry

    lax.fori_loop(0, 8, to_moved, 0, unroll=4)

    def to_out(i, carry):
        start = pl.multiple_of(i * 256, 256)
        total = lax.dot_general(
            moved_s[pl.ds(start, 256), :], wtd_s[...], (((1,), (1,)), ((), ())),
            preferred_element_type=f32,
        )
        total = (total * (2.0 / (SLOTS * BC * N_PAIR))).astype(bf16)
        for t in range(8):
            out_ref[t % N_X, 2 * i + t // N_X] = total[t * OWN:(t + 1) * OWN]
        return carry

    lax.fori_loop(0, 8, to_out, 0, unroll=4)


def shards(cond_orbitals, cond_energy, val_orbitals, val_energy, val_slots, owner_count):
    points = val_orbitals.reshape(N_KA, 2, GB).astype(f32)
    level = jnp.broadcast_to(val_energy.astype(f32)[:, None, None], (N_KA, 1, GB))
    wanted = jnp.pad(val_slots[0].astype(f32), ((0, 0), (0, GB - SLOTS)))
    wanted = jnp.broadcast_to(wanted[None], (N_KA, 5, GB))
    pieces = lax.all_to_all(jnp.concatenate([points, level, wanted], axis=1), "ka", 0, 0, tiled=True)
    slots = pieces[:, 3, :SLOTS].astype(jnp.int32)

    packed = pl.pallas_call(
        pack_kernel,
        out_shape=jax.ShapeDtypeStruct((N_PAIR, BLOCK, BC), bf16),
        in_specs=vmem(2),
        out_specs=vmem(1)[0],
        compiler_params=params(),
        name="pack",
    )(cond_orbitals[0], pieces)
    got = lax.all_to_all(packed, PAIR, 0, 0, tiled=True)

    picked = pl.pallas_call(
        pick_kernel,
        out_shape=jax.ShapeDtypeStruct((N_KA, 3, SLOTS, GB), bf16),
        in_specs=[pl.BlockSpec(memory_space=pltpu.SMEM)] + vmem(1),
        out_specs=vmem(1)[0],
        scratch_shapes=[
            pltpu.VMEM((N_PAIR, BLOCK - OWN, GB), f32),
            pltpu.VMEM((N_KA, 3, SLOTS, GB), f32),
        ],
        compiler_params=params(),
        name="pick",
    )(slots, got)
    picked = lax.all_to_all(picked, "ka", 0, 0, tiled=True)

    bd = jnp.kron(jnp.eye(2, dtype=f32), cosine_table(GB).astype(f32)).astype(bf16)
    ta = jnp.kron(cosine_table(GA).astype(f32), jnp.eye(16, dtype=f32)).astype(bf16)
    part = pl.pallas_call(
        owner_kernel,
        out_shape=jax.ShapeDtypeStruct((N_X, N_Y * N_ZH, OWN, WIN), bf16),
        in_specs=[pl.BlockSpec(memory_space=pltpu.SMEM)] + vmem(5),
        out_specs=vmem(1)[0],
        scratch_shapes=[
            pltpu.VMEM((GRID, PAIRS), bf16),
            pltpu.VMEM((GRID, PAIRS), bf16),
            pltpu.VMEM((WIN, PAIRS), bf16),
            pltpu.VMEM((SLOTS, BC), f32),
        ],
        compiler_params=params(),
        name="owner",
    )(owner_count[0], got, picked, cond_energy, bd, ta)

    part = lax.all_to_all(part, "x", 0, 0, tiled=True)
    part = jnp.sum(part.astype(f32), axis=0).astype(bf16)
    part = lax.all_to_all(part, ("y", "zh"), 0, 0, tiled=True)
    return jnp.sum(part.astype(f32), axis=0)[None]


def solution(mesh):
    mesh = Mesh(mesh.devices.reshape(N_KA, N_Y, N_ZH, N_X), ("ka", "y", "zh", "x"))
    return jax.shard_map(
        shards,
        mesh=mesh,
        in_specs=(
            P("ka", PAIR, None),
            P("ka", PAIR),
            P(("ka",) + PAIR, None),
            P(("ka",) + PAIR),
            P("ka", PAIR, None),
            P("ka", PAIR),
        ),
        out_specs=P("ka", PAIR, None),
        check_vma=False,
    )
```

time: 151 us -> 140 us (0.927)
  the two profiles are of different devices: /device:TPU:16 before, /device:TPU:2 now
where the time goes in v4:
time: 140 us; the launch traced here: 139 us
  blocking collectives  66.9 us (48%)
  waiting for transfers between devices  31.9 us (23%)
  starting transfers between devices  19.8 us (14%)
  Pallas kernels  13.7 us (10%)
  other arithmetic  3.31 us (2%)
  local copies, waits for them, and re-layouts  2.17 us (2%)
  between operations  1.42 us (1%)
    all_to_all x1, blocking collectives, shards(): part = lax.all_to_all(part, 'x', 0, 0, tiled=True)  29.7 us
    all_to_all x1, waiting for transfers between devices, shards(): got = lax.all_to_all(packed, PAIR, 0, 0, tiled=True)  26.9 us
    all_to_all x1, blocking collectives, shards(): part = lax.all_to_all(part, ('y', 'zh'), 0, 0, tiled=True)  24.4 us
    all_to_all x1, starting transfers between devices, shards(): got = lax.all_to_all(packed, PAIR, 0, 0, tiled=True)  16.4 us
    all_to_all x1, blocking collectives, shards(): lax.all_to_all(jnp.concatenate([points, level, wanted], axis=1), 'ka', 0,...  12.8 us
    pallas_call x1, Pallas kernels, shards(): pl.pallas_call(owner_kernel, out_shape=jax.ShapeDtypeStruct((N_X, N_Y * N...  10.8 us
    all_to_all x1, waiting for transfers between devices, shards(): picked = lax.all_to_all(picked, 'ka', 0, 0, tiled=True)  5.01 us
    all_to_all x1, starting transfers between devices, shards(): picked = lax.all_to_all(picked, 'ka', 0, 0, tiled=True)  3.36 us
  transfers between devices with their start and end apart: 2, of which 2 were waited for; matrix products, arithmetic and copies ran while one was open for 1% of the time, Pallas kernels for 0%

profile of v4, /device:TPU:2, one launch (start us, length us, event | category | flops | bytes accessed | tf_op | source)
XLA Modules:
  0.0 139.1 jit_solution(4929910796868754530)
XLA Ops:
  0.7 0.7 convert_bitcast_fusion
  1.3 0.7 convert_element_type.102
  2.0 0.1 pad.6.clone
  2.1 0.1 pad_maximum_fusion
  2.2 12.8 %all_to_all.25.pieces_ref = f32[8,8,128]{2,1,0:T(8,128)S(1)} all-to-all(f32[8,8,128]{2,1,0:T(8,128)S(1)} %pad_maximum_fusion), channel_id=1, replica_groups=mesh['ka'=8,'y'=8,'zh'=2,'x'=4] {'ka'}, dimensions={0} | all-to-all | bytes 65536 | tf_op jit(solution)/shard_map/all_to_all | solution.py:134
  15.0 0.0 copy-start
  15.0 1.0 copy-done
  16.0 1.0 pack.1
  17.1 16.4 %all-to-all-start.1 = ((bf16[64,56,128]{2,1,0:T(8,128)(2,1)}), bf16[64,56,128]{2,1,0:T(8,128)(2,1)S(1)}, u32[]{:S(2)}, u32[]{:S(2)}) async-start(bf16[64,56,128]{2,1,0:T(8,128)(2,1)} %pack.1), calls=%async_computation.1 | async-start | bytes 1835008 | tf_op jit(solution)/shard_map/all_to_all | solution.py:145
  33.5 0.0 copy-start.1
  34.2 0.2 fusion
  34.4 0.2 multiply_convert_fusion.1
  34.6 0.1 fusion.2
  34.7 26.9 %all-to-all-done.1.got_ref = bf16[64,56,128]{2,1,0:T(8,128)(2,1)S(1)} async-done(((bf16[64,56,128]{2,1,0:T(8,128)(2,1)}), bf16[64,56,128]{2,1,0:T(8,128)(2,1)S(1)}, u32[]{:S(2)}, u32[]{:S(2)}) %all-to-all-start.1) | async-done | bytes 917536 | tf_op jit(solution)/shard_map/all_to_all | solution.py:145
  61.6 1.8 %pick.1 = bf16[8,3,16,128]{3,2,1,0:T(8,128)(2,1)} custom-call(s32[8,16]{1,0:T(8,128)S(1)} %bitcast.24, bf16[64,56,128]{2,1,0:T(8,128)(2,1)S(1)} %all-to-all-done.1.got_ref), custom_call_target="tpu_custom_call" | custom-call | tf_op jit(solution)/shard_map/pick/pallas_call | solution.py:147
  63.4 3.4 %all-to-all-start.2 = ((bf16[8,3,16,128]{3,2,1,0:T(8,128)(2,1)}), bf16[8,3,16,128]{3,2,1,0:T(8,128)(2,1)S(1)}, u32[]{:S(2)}, u32[]{:S(2)}) async-start(bf16[8,3,16,128]{3,2,1,0:T(8,128)(2,1)} %pick.1), calls=%async_computation.2 | async-start | bytes 196608 | tf_op jit(solution)/shard_map/all_to_all | solution.py:159
  66.8 0.2 multiply_convert_fusion
  67.0 1.0 convert_element_type.100.ta_ref
  68.1 5.0 %all-to-all-done.2.pick_ref = bf16[8,3,16,128]{3,2,1,0:T(8,128)(2,1)S(1)} async-done(((bf16[8,3,16,128]{3,2,1,0:T(8,128)(2,1)}), bf16[8,3,16,128]{3,2,1,0:T(8,128)(2,1)S(1)}, u32[]{:S(2)}, u32[]{:S(2)}) %all-to-all-start.2) | async-done | bytes 98336 | tf_op jit(solution)/shard_map/all_to_all | solution.py:159
  73.1 0.0 copy-done.1
  73.1 10.8 %owner.1 = bf16[4,16,32,512]{3,2,1,0:T(8,128)(2,1)S(1)} custom-call(s32[1]{0:T(128)} %bitcast.21.count_ref, bf16[64,56,128]{2,1,0:T(8,128)(2,1)S(1)} %all-to-all-done.1.got_ref, bf16[8,3,16,128]{3,2,1,0:T(8,128)(2,1)S(1)} %all-to-all-done.2.pick_ref, f32[1,128]{1,0:T(1,128)S(1)} %copy-done.1, bf16[256,256]{1,0:T(8,128)(2,1)S(1)} %bitcast.23, ...), custom_call_target="tpu_custom_call" | custom-call | tf_op jit(solution)/shard_map/owner/pallas_call | solution.py:163
  83.9 29.7 %all_to_all.26 = bf16[4,16,32,512]{3,2,1,0:T(8,128)(2,1)S(1)} all-to-all(bf16[4,16,32,512]{3,2,1,0:T(8,128)(2,1)S(1)} %owner.1), channel_id=1, replica_groups=mesh['ka'=8,'y'=8,'zh'=2,'x'=4] {'x'}, dimensions={0} | all-to-all | bytes 4194304 | tf_op jit(solution)/shard_map/all_to_all | solution.py:178
  113.5 0.4 reduce_sum.21
  114.0 24.4 %all_to_all.27 = bf16[16,32,512]{2,1,0:T(8,128)(2,1)S(1)} all-to-all(bf16[16,32,512]{2,1,0:T(8,128)(2,1)S(1)} %reduce_sum.21), channel_id=1, replica_groups=mesh['ka'=8,'y'=8,'zh'=2,'x'=4] {'y','zh'}, dimensions={0} | all-to-all | bytes 1048576 | tf_op jit(solution)/shard_map/all_to_all | solution.py:180
  138.4 0.7 convert_reduce_fusion
  (8 shorter events, 0.1 us)
Async XLA Ops:
  15.0 1.0 copy-start
  17.1 44.5 %all-to-all-start.1 = ((bf16[64,56,128]{2,1,0:T(8,128)(2,1)}), bf16[64,56,128]{2,1,0:T(8,128)(2,1)S(1)}, u32[]{:S(2)}, u32[]{:S(2)}) async-start(bf16[64,56,128]{2,1,0:T(8,128)(2,1)} %pack.1), calls=%async_computation.1 | async-start | bytes 1835008 | tf_op jit(solution)/shard_map/all_to_all | solution.py:145
  33.5 39.6 %copy-start.1 = (f32[1,128]{1,0:T(1,128)S(1)}, f32[1,128]{1,0:T(1,128)}, u32[]{:S(2)}) copy-start(f32[1,128]{1,0:T(1,128)} %e_cond_ref.1) | copy-start | bytes 1540
  63.4 9.6 %all-to-all-start.2 = ((bf16[8,3,16,128]{3,2,1,0:T(8,128)(2,1)}), bf16[8,3,16,128]{3,2,1,0:T(8,128)(2,1)S(1)}, u32[]{:S(2)}, u32[]{:S(2)}) async-start(bf16[8,3,16,128]{3,2,1,0:T(8,128)(2,1)} %pick.1), calls=%async_computation.2 | async-start | bytes 196608 | tf_op jit(solution)/shard_map/all_to_all | solution.py:159

commit v5 on v4

--- a/solution.py
+++ b/solution.py
@@ -14,7 +14,8 @@
 NC = 8192
 N_KA = 8
 N_PAIR = 64
-N_Y = 8
+N_YH = 4
+N_YL = 2
 N_ZH = 2
 N_X = 4
 OWN = GRID // N_PAIR
@@ -23,7 +24,9 @@
 BLOCK = OWN + 2 * N_KA + N_KA
 ENERGY = OWN + 2 * N_KA
 
-PAIR = ("y", "zh", "x")
+PAIR = ("yh", "yl", "zh", "x")
+NEAR = ("yl", "x")
+FAR = ("yh", "zh")
 
 f32 = jnp.float32
 bf16 = jnp.bfloat16
@@ -120,7 +123,9 @@
         )
         total = (total * (2.0 / (SLOTS * BC * N_PAIR))).astype(bf16)
         for t in range(8):
-            out_ref[t % N_X, 2 * i + t // N_X] = total[t * OWN:(t + 1) * OWN]
+            near = lax.rem(i, N_YL) * N_X + t % N_X
+            far = lax.div(i, N_YL) * N_ZH + t // N_X
+            out_ref[near, far] = total[t * OWN:(t + 1) * OWN]
         return carry
 
     lax.fori_loop(0, 8, to_out, 0, unroll=4)
@@ -162,7 +167,7 @@
     ta = jnp.kron(cosine_table(GA).astype(f32), jnp.eye(16, dtype=f32)).astype(bf16)
     part = pl.pallas_call(
         owner_kernel,
-        out_shape=jax.ShapeDtypeStruct((N_X, N_Y * N_ZH, OWN, WIN), bf16),
+        out_shape=jax.ShapeDtypeStruct((N_YL * N_X, N_YH * N_ZH, OWN, WIN), bf16),
         in_specs=[pl.BlockSpec(memory_space=pltpu.SMEM)] + vmem(5),
         out_specs=vmem(1)[0],
         scratch_shapes=[
@@ -175,14 +180,14 @@
         name="owner",
     )(owner_count[0], got, picked, cond_energy, bd, ta)
 
-    part = lax.all_to_all(part, "x", 0, 0, tiled=True)
+    part = lax.all_to_all(part, NEAR, 0, 0, tiled=True)
     part = jnp.sum(part.astype(f32), axis=0).astype(bf16)
-    part = lax.all_to_all(part, ("y", "zh"), 0, 0, tiled=True)
+    part = lax.all_to_all(part, FAR, 0, 0, tiled=True)
     return jnp.sum(part.astype(f32), axis=0)[None]
 
 
 def solution(mesh):
-    mesh = Mesh(mesh.devices.reshape(N_KA, N_Y, N_ZH, N_X), ("ka", "y", "zh", "x"))
+    mesh = Mesh(mesh.devices.reshape(N_KA, N_YH, N_YL, N_ZH, N_X), ("ka",) + PAIR)
     return jax.shard_map(
         shards,
         mesh=mesh,

time: 140 us -> 134 us (0.957)
  the two profiles are of different devices: /device:TPU:2 before, /device:TPU:16 now
where the time goes in v5:
time: 134 us; the launch traced here: 133 us
  blocking collectives  62 us (46%)
  waiting for transfers between devices  31.4 us (23%)
  starting transfers between devices  19.6 us (15%)
  Pallas kernels  13.7 us (10%)
  other arithmetic  3.24 us (2%)
  local copies, waits for them, and re-layouts  2.17 us (2%)
  between operations  1.42 us (1%)
    all_to_all x1, blocking collectives, shards(): part = lax.all_to_all(part, NEAR, 0, 0, tiled=True)  30.9 us
    all_to_all x1, waiting for transfers between devices, shards(): got = lax.all_to_all(packed, PAIR, 0, 0, tiled=True)  26.4 us
    all_to_all x1, blocking collectives, shards(): part = lax.all_to_all(part, FAR, 0, 0, tiled=True)  18.2 us
    all_to_all x1, starting transfers between devices, shards(): got = lax.all_to_all(packed, PAIR, 0, 0, tiled=True)  16.2 us
    all_to_all x1, blocking collectives, shards(): lax.all_to_all(jnp.concatenate([points, level, wanted], axis=1), 'ka', 0,...  12.8 us
    pallas_call x1, Pallas kernels, shards(): pl.pallas_call(owner_kernel, out_shape=jax.ShapeDtypeStruct((N_YL * N_X,...  10.8 us
    all_to_all x1, waiting for transfers between devices, shards(): picked = lax.all_to_all(picked, 'ka', 0, 0, tiled=True)  5.01 us
    all_to_all x1, starting transfers between devices, shards(): picked = lax.all_to_all(picked, 'ka', 0, 0, tiled=True)  3.36 us
  transfers between devices with their start and end apart: 2, of which 2 were waited for; matrix products, arithmetic and copies ran while one was open for 1% of the time, Pallas kernels for 0%

profile of v5, /device:TPU:16, one launch (start us, length us, event | category | flops | bytes accessed | tf_op | source)
XLA Modules:
  0.0 133.4 jit_solution(4847395266298185160)
XLA Ops:
  0.7 0.7 convert_bitcast_fusion
  1.3 0.7 convert_element_type.102
  2.0 0.1 pad.6.clone
  2.1 0.1 pad_maximum_fusion
  2.2 12.8 %all_to_all.25.pieces_ref = f32[8,8,128]{2,1,0:T(8,128)S(1)} all-to-all(f32[8,8,128]{2,1,0:T(8,128)S(1)} %pad_maximum_fusion), channel_id=1, replica_groups=mesh['ka'=8,'yh'=4,'yl'=2,'zh'=2,'x'=4] {'ka'}, dimensions={0} | all-to-all | bytes 65536 | tf_op jit(solution)/shard_map/all_to_all | solution.py:139
  15.0 0.0 copy-start
  15.0 1.0 copy-done
  16.0 1.0 pack.1
  17.1 16.2 %all-to-all-start.1 = ((bf16[64,56,128]{2,1,0:T(8,128)(2,1)}), bf16[64,56,128]{2,1,0:T(8,128)(2,1)S(1)}, u32[]{:S(2)}, u32[]{:S(2)}) async-start(bf16[64,56,128]{2,1,0:T(8,128)(2,1)} %pack.1), calls=%async_computation.1 | async-start | bytes 1835008 | tf_op jit(solution)/shard_map/all_to_all | solution.py:150
  33.3 0.0 copy-start.1
  34.0 0.2 fusion
  34.2 0.2 multiply_convert_fusion.1
  34.4 0.1 fusion.2
  34.5 26.4 %all-to-all-done.1.got_ref = bf16[64,56,128]{2,1,0:T(8,128)(2,1)S(1)} async-done(((bf16[64,56,128]{2,1,0:T(8,128)(2,1)}), bf16[64,56,128]{2,1,0:T(8,128)(2,1)S(1)}, u32[]{:S(2)}, u32[]{:S(2)}) %all-to-all-start.1) | async-done | bytes 917536 | tf_op jit(solution)/shard_map/all_to_all | solution.py:150
  60.9 1.8 %pick.1 = bf16[8,3,16,128]{3,2,1,0:T(8,128)(2,1)} custom-call(s32[8,16]{1,0:T(8,128)S(1)} %bitcast.24, bf16[64,56,128]{2,1,0:T(8,128)(2,1)S(1)} %all-to-all-done.1.got_ref), custom_call_target="tpu_custom_call" | custom-call | tf_op jit(solution)/shard_map/pick/pallas_call | solution.py:152
  62.7 3.4 %all-to-all-start.2 = ((bf16[8,3,16,128]{3,2,1,0:T(8,128)(2,1)}), bf16[8,3,16,128]{3,2,1,0:T(8,128)(2,1)S(1)}, u32[]{:S(2)}, u32[]{:S(2)}) async-start(bf16[8,3,16,128]{3,2,1,0:T(8,128)(2,1)} %pick.1), calls=%async_computation.2 | async-start | bytes 196608 | tf_op jit(solution)/shard_map/all_to_all | solution.py:164
  66.1 0.2 multiply_convert_fusion
  66.4 1.0 convert_element_type.100.ta_ref
  67.4 5.0 %all-to-all-done.2.pick_ref = bf16[8,3,16,128]{3,2,1,0:T(8,128)(2,1)S(1)} async-done(((bf16[8,3,16,128]{3,2,1,0:T(8,128)(2,1)}), bf16[8,3,16,128]{3,2,1,0:T(8,128)(2,1)S(1)}, u32[]{:S(2)}, u32[]{:S(2)}) %all-to-all-start.2) | async-done | bytes 98336 | tf_op jit(solution)/shard_map/all_to_all | solution.py:164
  72.4 0.0 copy-done.1
  72.4 10.8 %owner.1 = bf16[8,8,32,512]{3,2,1,0:T(8,128)(2,1)S(1)} custom-call(s32[1]{0:T(128)} %bitcast.21.count_ref, bf16[64,56,128]{2,1,0:T(8,128)(2,1)S(1)} %all-to-all-done.1.got_ref, bf16[8,3,16,128]{3,2,1,0:T(8,128)(2,1)S(1)} %all-to-all-done.2.pick_ref, f32[1,128]{1,0:T(1,128)S(1)} %copy-done.1, bf16[256,256]{1,0:T(8,128)(2,1)S(1)} %bitcast.23, ...), custom_call_target="tpu_custom_call" | custom-call | tf_op jit(solution)/shard_map/owner/pallas_call | solution.py:168
  83.2 30.9 %all_to_all.26 = bf16[8,8,32,512]{3,2,1,0:T(8,128)(2,1)S(1)} all-to-all(bf16[8,8,32,512]{3,2,1,0:T(8,128)(2,1)S(1)} %owner.1), channel_id=1, replica_groups=mesh['ka'=8,'yh'=4,'yl'=2,'zh'=2,'x'=4] {'yl','x'}, dimensions={0} | all-to-all | bytes 4194304 | tf_op jit(solution)/shard_map/all_to_all | solution.py:183
  114.1 0.4 reduce_sum.21
  114.5 18.2 %all_to_all.27 = bf16[8,32,512]{2,1,0:T(8,128)(2,1)S(1)} all-to-all(bf16[8,32,512]{2,1,0:T(8,128)(2,1)S(1)} %reduce_sum.21), channel_id=1, replica_groups=mesh['ka'=8,'yh'=4,'yl'=2,'zh'=2,'x'=4] {'yh','zh'}, dimensions={0} | all-to-all | bytes 524288 | tf_op jit(solution)/shard_map/all_to_all | solution.py:185
  132.8 0.7 convert_reduce_fusion
  (8 shorter events, 0.1 us)
Async XLA Ops:
  15.0 1.0 copy-start
  17.1 43.8 %all-to-all-start.1 = ((bf16[64,56,128]{2,1,0:T(8,128)(2,1)}), bf16[64,56,128]{2,1,0:T(8,128)(2,1)S(1)}, u32[]{:S(2)}, u32[]{:S(2)}) async-start(bf16[64,56,128]{2,1,0:T(8,128)(2,1)} %pack.1), calls=%async_computation.1 | async-start | bytes 1835008 | tf_op jit(solution)/shard_map/all_to_all | solution.py:150
  33.3 39.1 %copy-start.1 = (f32[1,128]{1,0:T(1,128)S(1)}, f32[1,128]{1,0:T(1,128)}, u32[]{:S(2)}) copy-start(f32[1,128]{1,0:T(1,128)} %e_cond_ref.1) | copy-start | bytes 1540
  62.7 9.6 %all-to-all-start.2 = ((bf16[8,3,16,128]{3,2,1,0:T(8,128)(2,1)}), bf16[8,3,16,128]{3,2,1,0:T(8,128)(2,1)S(1)}, u32[]{:S(2)}, u32[]{:S(2)}) async-start(bf16[8,3,16,128]{3,2,1,0:T(8,128)(2,1)} %pick.1), calls=%async_computation.2 | async-start | bytes 196608 | tf_op jit(solution)/shard_map/all_to_all | solution.py:164

commit v6 on v5

--- a/solution.py
+++ b/solution.py
@@ -47,11 +47,16 @@
     return pltpu.CompilerParams(vmem_limit_bytes=48 * 2**20)
 
 
-def pack_kernel(cond_ref, pieces_ref, out_ref):
+def cond_kernel(cond_ref, out_ref):
+    for d in range(N_PAIR):
+        out_ref[d] = cond_ref[:, d * BC:(d + 1) * BC]
+
+
+def pack_kernel(pieces_ref, cond_ref, out_ref):
     points = jnp.concatenate([pieces_ref[k, :2, :] for k in range(N_KA)], axis=0).astype(bf16)
     levels = jnp.concatenate([pieces_ref[k, 2:3, :] for k in range(N_KA)], axis=0).astype(bf16)
     for d in range(N_PAIR):
-        out_ref[d, :OWN, :] = cond_ref[:, d * BC:(d + 1) * BC]
+        out_ref[d, :OWN, :] = cond_ref[d]
         out_ref[d, OWN:ENERGY, :] = points
         out_ref[d, ENERGY:, :] = levels
 
@@ -62,8 +67,8 @@
     for k in range(N_KA):
         for s in range(SLOTS):
             slot = slots_ref[k, s]
-            owner = lax.rem(slot, N_PAIR)
-            line = lax.div(slot, N_PAIR)
+            owner = jnp.bitwise_and(slot, N_PAIR - 1)
+            line = lax.shift_right_logical(slot, 6)
             for a in range(2):
                 picked_s[k, a, s:s + 1, :] = rows_s[owner, pl.ds(2 * line + a, 1), :]
             picked_s[k, 2, s:s + 1, :] = rows_s[owner, pl.ds(2 * N_KA + line, 1), :]
@@ -94,7 +99,7 @@
                     first_s[pl.ds(at, 16), s0 * BC:(s0 + GROUP) * BC] = first[row:row + 16, :]
         return carry
 
-    lax.fori_loop(0, 8, to_first, 0, unroll=4)
+    lax.fori_loop(0, 8, to_first, 0, unroll=8)
 
     def to_moved(kg, carry):
         start = pl.multiple_of(kg * 256, 256)
@@ -113,7 +118,7 @@
                         wtd_s[pl.ds(at, 16), s * BC:(s + 1) * BC] = part.astype(bf16)
         return carry
 
-    lax.fori_loop(0, 8, to_moved, 0, unroll=4)
+    lax.fori_loop(0, 8, to_moved, 0, unroll=8)
 
     def to_out(i, carry):
         start = pl.multiple_of(i * 256, 256)
@@ -128,7 +133,7 @@
             out_ref[near, far] = total[t * OWN:(t + 1) * OWN]
         return carry
 
-    lax.fori_loop(0, 8, to_out, 0, unroll=4)
+    lax.fori_loop(0, 8, to_out, 0, unroll=8)
 
 
 def shards(cond_orbitals, cond_energy, val_orbitals, val_energy, val_slots, owner_count):
@@ -139,6 +144,14 @@
     pieces = lax.all_to_all(jnp.concatenate([points, level, wanted], axis=1), "ka", 0, 0, tiled=True)
     slots = pieces[:, 3, :SLOTS].astype(jnp.int32)
 
+    cond = pl.pallas_call(
+        cond_kernel,
+        out_shape=jax.ShapeDtypeStruct((N_PAIR, OWN, BC), bf16),
+        in_specs=vmem(1),
+        out_specs=vmem(1)[0],
+        compiler_params=params(),
+        name="cond",
+    )(cond_orbitals[0])
     packed = pl.pallas_call(
         pack_kernel,
         out_shape=jax.ShapeDtypeStruct((N_PAIR, BLOCK, BC), bf16),
@@ -146,7 +159,7 @@
         out_specs=vmem(1)[0],
         compiler_params=params(),
         name="pack",
-    )(cond_orbitals[0], pieces)
+    )(pieces, cond)
     got = lax.all_to_all(packed, PAIR, 0, 0, tiled=True)
 
     picked = pl.pallas_call(

time: 134 us -> 134 us (level)
  blocking collectives: 62 us -> 49.3 us
  starting transfers between devices: 19.6 us -> 27 us
  waiting for transfers between devices: 31.4 us -> 35.8 us
    all_to_all x1 -> x0, blocking collectives: 12.8 us -> none  [shards(): lax.all_to_all(jnp.concatenate([points, level, wanted], axis=1), 'ka', 0,...]
    all_to_all x0 -> x1, starting transfers between devices: none -> 7.27 us  [shards(): lax.all_to_all(jnp.concatenate([points, level, wanted], axis=1), 'ka', 0,...]
    all_to_all x0 -> x1, waiting for transfers between devices: none -> 4.61 us  [shards(): lax.all_to_all(jnp.concatenate([points, level, wanted], axis=1), 'ka', 0,...]
  transfers between devices with their start and end apart: 2 -> 3, of which waited for: 2 -> 3; matrix products, arithmetic and copies ran while one was open for 1% -> 1% of each run, Pallas kernels for 0% -> 0%
where the time goes in v6:
time: 134 us; the launch traced here: 133 us
  blocking collectives  49.3 us (37%)
  waiting for transfers between devices  35.8 us (27%)
  starting transfers between devices  27 us (20%)
  Pallas kernels  13.8 us (10%)
  other arithmetic  3.85 us (3%)
  local copies, waits for them, and re-layouts  2.17 us (2%)
  between operations  1.43 us (1%)
    all_to_all x1, blocking collectives, shards(): part = lax.all_to_all(part, NEAR, 0, 0, tiled=True)  30.9 us
    all_to_all x1, waiting for transfers between devices, shards(): got = lax.all_to_all(packed, PAIR, 0, 0, tiled=True)  26.4 us
    all_to_all x1, blocking collectives, shards(): part = lax.all_to_all(part, FAR, 0, 0, tiled=True)  18.3 us
    all_to_all x1, starting transfers between devices, shards(): got = lax.all_to_all(packed, PAIR, 0, 0, tiled=True)  16.2 us
    pallas_call x1, Pallas kernels, shards(): pl.pallas_call(owner_kernel, out_shape=jax.ShapeDtypeStruct((N_YL * N_X,...  11.1 us
    all_to_all x1, starting transfers between devices, shards(): lax.all_to_all(jnp.concatenate([points, level, wanted], axis=1), 'ka', 0,...  7.27 us
    all_to_all x1, waiting for transfers between devices, shards(): picked = lax.all_to_all(picked, 'ka', 0, 0, tiled=True)  4.83 us
    all_to_all x1, waiting for transfers between devices, shards(): lax.all_to_all(jnp.concatenate([points, level, wanted], axis=1), 'ka', 0,...  4.61 us
  transfers between devices with their start and end apart: 3, of which 3 were waited for; matrix products, arithmetic and copies ran while one was open for 1% of the time, Pallas kernels for 0%

profile of v6, /device:TPU:16, one launch (start us, length us, event | category | flops | bytes accessed | tf_op | source)
XLA Modules:
  0.0 133.3 jit_solution(18435571816081026924)
XLA Ops:
  0.7 0.7 convert_bitcast_fusion
  1.3 0.7 convert_element_type.102
  2.0 0.1 pad.6.clone
  2.1 0.7 pad_maximum_fusion
  2.8 7.3 %all-to-all-start = ((f32[8,8,128]{2,1,0:T(8,128)}), f32[8,8,128]{2,1,0:T(8,128)S(1)}, u32[]{:S(2)}, u32[]{:S(2)}) async-start(f32[8,8,128]{2,1,0:T(8,128)} %pad_maximum_fusion), calls=%async_computation | async-start | bytes 65536 | tf_op jit(solution)/shard_map/all_to_all | solution.py:144
  10.1 0.0 copy-start
  10.1 1.0 copy-done
  11.1 0.1 cond.1.cond_ref
  11.2 4.6 %all-to-all-done.pieces_ref = f32[8,8,128]{2,1,0:T(8,128)S(1)} async-done(((f32[8,8,128]{2,1,0:T(8,128)}), f32[8,8,128]{2,1,0:T(8,128)S(1)}, u32[]{:S(2)}, u32[]{:S(2)}) %all-to-all-start) | async-done | bytes 32800 | tf_op jit(solution)/shard_map/all_to_all | solution.py:144
  15.8 1.0 pack.1
  16.8 16.2 %all-to-all-start.1 = ((bf16[64,56,128]{2,1,0:T(8,128)(2,1)}), bf16[64,56,128]{2,1,0:T(8,128)(2,1)S(1)}, u32[]{:S(2)}, u32[]{:S(2)}) async-start(bf16[64,56,128]{2,1,0:T(8,128)(2,1)} %pack.1), calls=%async_computation.1 | async-start | bytes 1835008 | tf_op jit(solution)/shard_map/all_to_all | solution.py:163
  33.0 0.0 copy-start.1
  33.7 0.2 fusion
  34.0 0.2 multiply_convert_fusion.1
  34.2 0.1 fusion.2
  34.3 26.4 %all-to-all-done.1.got_ref = bf16[64,56,128]{2,1,0:T(8,128)(2,1)S(1)} async-done(((bf16[64,56,128]{2,1,0:T(8,128)(2,1)}), bf16[64,56,128]{2,1,0:T(8,128)(2,1)S(1)}, u32[]{:S(2)}, u32[]{:S(2)}) %all-to-all-start.1) | async-done | bytes 917536 | tf_op jit(solution)/shard_map/all_to_all | solution.py:163
  60.6 1.6 %pick.1 = bf16[8,3,16,128]{3,2,1,0:T(8,128)(2,1)} custom-call(s32[8,16]{1,0:T(8,128)S(1)} %bitcast.24, bf16[64,56,128]{2,1,0:T(8,128)(2,1)S(1)} %all-to-all-done.1.got_ref), custom_call_target="tpu_custom_call" | custom-call | tf_op jit(solution)/shard_map/pick/pallas_call | solution.py:165
  62.3 3.5 %all-to-all-start.2 = ((bf16[8,3,16,128]{3,2,1,0:T(8,128)(2,1)}), bf16[8,3,16,128]{3,2,1,0:T(8,128)(2,1)S(1)}, u32[]{:S(2)}, u32[]{:S(2)}) async-start(bf16[8,3,16,128]{3,2,1,0:T(8,128)(2,1)} %pick.1), calls=%async_computation.2 | async-start | bytes 196608 | tf_op jit(solution)/shard_map/all_to_all | solution.py:177
  65.8 0.2 multiply_convert_fusion
  66.1 1.0 convert_element_type.100.ta_ref
  67.1 4.8 %all-to-all-done.2.pick_ref = bf16[8,3,16,128]{3,2,1,0:T(8,128)(2,1)S(1)} async-done(((bf16[8,3,16,128]{3,2,1,0:T(8,128)(2,1)}), bf16[8,3,16,128]{3,2,1,0:T(8,128)(2,1)S(1)}, u32[]{:S(2)}, u32[]{:S(2)}) %all-to-all-start.2) | async-done | bytes 98336 | tf_op jit(solution)/shard_map/all_to_all | solution.py:177
  71.9 0.0 copy-done.1
  71.9 11.1 %owner.1 = bf16[8,8,32,512]{3,2,1,0:T(8,128)(2,1)S(1)} custom-call(s32[1]{0:T(128)} %bitcast.21.count_ref, bf16[64,56,128]{2,1,0:T(8,128)(2,1)S(1)} %all-to-all-done.1.got_ref, bf16[8,3,16,128]{3,2,1,0:T(8,128)(2,1)S(1)} %all-to-all-done.2.pick_ref, f32[1,128]{1,0:T(1,128)S(1)} %copy-done.1, bf16[256,256]{1,0:T(8,128)(2,1)S(1)} %bitcast.22, ...), custom_call_target="tpu_custom_call" | custom-call | tf_op jit(solution)/shard_map/owner/pallas_call | solution.py:181
  83.0 30.9 %all_to_all.25 = bf16[8,8,32,512]{3,2,1,0:T(8,128)(2,1)S(1)} all-to-all(bf16[8,8,32,512]{3,2,1,0:T(8,128)(2,1)S(1)} %owner.1), channel_id=1, replica_groups=mesh['ka'=8,'yh'=4,'yl'=2,'zh'=2,'x'=4] {'yl','x'}, dimensions={0} | all-to-all | bytes 4194304 | tf_op jit(solution)/shard_map/all_to_all | solution.py:196
  113.9 0.4 reduce_sum.21
  114.3 18.3 %all_to_all.26 = bf16[8,32,512]{2,1,0:T(8,128)(2,1)S(1)} all-to-all(bf16[8,32,512]{2,1,0:T(8,128)(2,1)S(1)} %reduce_sum.21), channel_id=1, replica_groups=mesh['ka'=8,'yh'=4,'yl'=2,'zh'=2,'x'=4] {'yh','zh'}, dimensions={0} | all-to-all | bytes 524288 | tf_op jit(solution)/shard_map/all_to_all | solution.py:198
  132.7 0.7 convert_reduce_fusion
  (8 shorter events, 0.1 us)
Async XLA Ops:
  2.8 13.0 %all-to-all-start = ((f32[8,8,128]{2,1,0:T(8,128)}), f32[8,8,128]{2,1,0:T(8,128)S(1)}, u32[]{:S(2)}, u32[]{:S(2)}) async-start(f32[8,8,128]{2,1,0:T(8,128)} %pad_maximum_fusion), calls=%async_computation | async-start | bytes 65536 | tf_op jit(solution)/shard_map/all_to_all | solution.py:144
  10.1 1.0 copy-start
  16.8 43.8 %all-to-all-start.1 = ((bf16[64,56,128]{2,1,0:T(8,128)(2,1)}), bf16[64,56,128]{2,1,0:T(8,128)(2,1)S(1)}, u32[]{:S(2)}, u32[]{:S(2)}) async-start(bf16[64,56,128]{2,1,0:T(8,128)(2,1)} %pack.1), calls=%async_computation.1 | async-start | bytes 1835008 | tf_op jit(solution)/shard_map/all_to_all | solution.py:163
  33.0 38.9 %copy-start.1 = (f32[1,128]{1,0:T(1,128)S(1)}, f32[1,128]{1,0:T(1,128)}, u32[]{:S(2)}) copy-start(f32[1,128]{1,0:T(1,128)} %e_cond_ref.1) | copy-start | bytes 1540
  62.3 9.6 %all-to-all-start.2 = ((bf16[8,3,16,128]{3,2,1,0:T(8,128)(2,1)}), bf16[8,3,16,128]{3,2,1,0:T(8,128)(2,1)S(1)}, u32[]{:S(2)}, u32[]{:S(2)}) async-start(bf16[8,3,16,128]{3,2,1,0:T(8,128)(2,1)} %pick.1), calls=%async_computation.2 | async-start | bytes 196608 | tf_op jit(solution)/shard_map/all_to_all | solution.py:177

commit v7 on v6

--- a/solution.py
+++ b/solution.py
@@ -47,6 +47,26 @@
     return pltpu.CompilerParams(vmem_limit_bytes=48 * 2**20)
 
 
+def piece_kernel(energy_ref, val_ref, slots_ref, out_ref, val_s, slots_s, sems):
+    copies = [
+        pltpu.make_async_copy(val_ref, val_s, sems.at[0]),
+        pltpu.make_async_copy(slots_ref, slots_s, sems.at[1]),
+    ]
+    for copy in copies:
+        copy.start()
+    out_ref[...] = jnp.zeros_like(out_ref)
+    for k in range(N_KA):
+        out_ref[k, 2:3, :] = energy_ref[:1, :].astype(f32)
+    for copy in copies:
+        copy.wait()
+    wanted = slots_s[...].astype(f32)
+    for k in range(N_KA):
+        for a in range(2):
+            at = (2 * k + a) * GB
+            out_ref[k, a:a + 1, :] = val_s[:, at:at + GB].astype(f32)
+        out_ref[k, 3:4, :SLOTS] = wanted
+
+
 def cond_kernel(cond_ref, out_ref):
     for d in range(N_PAIR):
         out_ref[d] = cond_ref[:, d * BC:(d + 1) * BC]
@@ -99,7 +119,7 @@
                     first_s[pl.ds(at, 16), s0 * BC:(s0 + GROUP) * BC] = first[row:row + 16, :]
         return carry
 
-    lax.fori_loop(0, 8, to_first, 0, unroll=8)
+    lax.fori_loop(0, 8, to_first, 0, unroll=4)
 
     def to_moved(kg, carry):
         start = pl.multiple_of(kg * 256, 256)
@@ -118,7 +138,7 @@
                         wtd_s[pl.ds(at, 16), s * BC:(s + 1) * BC] = part.astype(bf16)
         return carry
 
-    lax.fori_loop(0, 8, to_moved, 0, unroll=8)
+    lax.fori_loop(0, 8, to_moved, 0, unroll=4)
 
     def to_out(i, carry):
         start = pl.multiple_of(i * 256, 256)
@@ -133,15 +153,24 @@
             out_ref[near, far] = total[t * OWN:(t + 1) * OWN]
         return carry
 
-    lax.fori_loop(0, 8, to_out, 0, unroll=8)
+    lax.fori_loop(0, 8, to_out, 0, unroll=4)
 
 
 def shards(cond_orbitals, cond_energy, val_orbitals, val_energy, val_slots, owner_count):
-    points = val_orbitals.reshape(N_KA, 2, GB).astype(f32)
-    level = jnp.broadcast_to(val_energy.astype(f32)[:, None, None], (N_KA, 1, GB))
-    wanted = jnp.pad(val_slots[0].astype(f32), ((0, 0), (0, GB - SLOTS)))
-    wanted = jnp.broadcast_to(wanted[None], (N_KA, 5, GB))
-    pieces = lax.all_to_all(jnp.concatenate([points, level, wanted], axis=1), "ka", 0, 0, tiled=True)
+    pieces = pl.pallas_call(
+        piece_kernel,
+        out_shape=jax.ShapeDtypeStruct((N_KA, 8, GB), f32),
+        in_specs=vmem(1) + [pl.BlockSpec(memory_space=pl.ANY)] * 2,
+        out_specs=vmem(1)[0],
+        scratch_shapes=[
+            pltpu.VMEM((1, GRID), bf16),
+            pltpu.VMEM((1, SLOTS), jnp.int32),
+            pltpu.SemaphoreType.DMA((2,)),
+        ],
+        compiler_params=pltpu.CompilerParams(vmem_limit_bytes=60 * 2**20),
+        name="piece",
+    )(jnp.broadcast_to(val_energy[:, None], (8, GB)), val_orbitals, val_slots[0])
+    pieces = lax.all_to_all(pieces, "ka", 0, 0, tiled=True)
     slots = pieces[:, 3, :SLOTS].astype(jnp.int32)
 
     cond = pl.pallas_call(

time: 134 us -> 134 us (level)
  other arithmetic: 3.85 us -> 1.81 us
  Pallas kernels: 13.8 us -> 15.7 us
    pallas_call x0 -> x1, Pallas kernels: none -> 2 us  [shards(): pl.pallas_call(piece_kernel, out_shape=jax.ShapeDtypeStruct((N_KA, 8, GB)...]
    convert_element_type x2 -> x0, other arithmetic: 1.36 us -> none  [the longest x1 0.71 us: shards(): points = val_orbitals.reshape(N_KA, 2, GB).astype(f32)]
where the time goes in v7:
time: 134 us
  blocking collectives  49.2 us (37%)
  waiting for transfers between devices  36 us (27%)
  starting transfers between devices  26.8 us (20%)
  Pallas kernels  15.7 us (12%)
  local copies, waits for them, and re-layouts  2.66 us (2%)
  other arithmetic  1.81 us (1%)
  between operations  1.43 us (1%)
    all_to_all x1, blocking collectives, shards(): part = lax.all_to_all(part, NEAR, 0, 0, tiled=True)  30.9 us
    all_to_all x1, waiting for transfers between devices, shards(): got = lax.all_to_all(packed, PAIR, 0, 0, tiled=True)  26.4 us
    all_to_all x1, blocking collectives, shards(): part = lax.all_to_all(part, FAR, 0, 0, tiled=True)  18.2 us
    all_to_all x1, starting transfers between devices, shards(): got = lax.all_to_all(packed, PAIR, 0, 0, tiled=True)  16.2 us
    pallas_call x1, Pallas kernels, shards(): pl.pallas_call(owner_kernel, out_shape=jax.ShapeDtypeStruct((N_YL * N_X,...  10.9 us
    all_to_all x1, starting transfers between devices, shards(): pieces = lax.all_to_all(pieces, 'ka', 0, 0, tiled=True)  7.28 us
    all_to_all x1, waiting for transfers between devices, shards(): picked = lax.all_to_all(picked, 'ka', 0, 0, tiled=True)  5.01 us
    all_to_all x1, waiting for transfers between devices, shards(): pieces = lax.all_to_all(pieces, 'ka', 0, 0, tiled=True)  4.61 us
  transfers between devices with their start and end apart: 3, of which 3 were waited for; matrix products, arithmetic and copies ran while one was open for 1% of the time, Pallas kernels for 0%

profile of v7, /device:TPU:16, one launch (start us, length us, event | category | flops | bytes accessed | tf_op | source)
XLA Modules:
  0.0 133.6 jit_solution(291722325496588999)
XLA Ops:
  0.7 0.6 broadcast_in_dim.40.energy_ref
  1.2 2.0 %piece.1 = f32[8,8,128]{2,1,0:T(8,128)} custom-call(bf16[8,128]{1,0:T(8,128)(2,1)} %broadcast_in_dim.40.energy_ref, bf16[1,2048]{1,0:T(2,128)(2,1)} %val_ref.1, s32[1,16]{1,0:T(1,128)} %bitcast.19), custom_call_target="tpu_custom_call" | custom-call | tf_op jit(solution)/shard_map/piece/pallas_call | solution.py:160
  3.2 7.3 %all-to-all-start = ((f32[8,8,128]{2,1,0:T(8,128)}), f32[8,8,128]{2,1,0:T(8,128)S(1)}, u32[]{:S(2)}, u32[]{:S(2)}) async-start(f32[8,8,128]{2,1,0:T(8,128)} %piece.1), calls=%async_computation | async-start | bytes 65536 | tf_op jit(solution)/shard_map/all_to_all | solution.py:173
  10.5 0.0 copy-start
  10.5 1.0 copy-done
  11.6 0.1 cond.1.cond_ref
  11.7 4.6 %all-to-all-done.pieces_ref = f32[8,8,128]{2,1,0:T(8,128)S(1)} async-done(((f32[8,8,128]{2,1,0:T(8,128)}), f32[8,8,128]{2,1,0:T(8,128)S(1)}, u32[]{:S(2)}, u32[]{:S(2)}) %all-to-all-start) | async-done | bytes 32800 | tf_op jit(solution)/shard_map/all_to_all | solution.py:173
  16.3 1.0 pack.1
  17.3 16.2 %all-to-all-start.1 = ((bf16[64,56,128]{2,1,0:T(8,128)(2,1)}), bf16[64,56,128]{2,1,0:T(8,128)(2,1)S(1)}, u32[]{:S(2)}, u32[]{:S(2)}) async-start(bf16[64,56,128]{2,1,0:T(8,128)(2,1)} %pack.1), calls=%async_computation.1 | async-start | bytes 1835008 | tf_op jit(solution)/shard_map/all_to_all | solution.py:192
  33.5 0.0 copy-start.1
  34.2 0.2 fusion
  34.4 0.2 multiply_convert_fusion.1
  34.6 0.1 fusion.2
  34.7 26.4 %all-to-all-done.1.got_ref = bf16[64,56,128]{2,1,0:T(8,128)(2,1)S(1)} async-done(((bf16[64,56,128]{2,1,0:T(8,128)(2,1)}), bf16[64,56,128]{2,1,0:T(8,128)(2,1)S(1)}, u32[]{:S(2)}, u32[]{:S(2)}) %all-to-all-start.1) | async-done | bytes 917536 | tf_op jit(solution)/shard_map/all_to_all | solution.py:192
  61.1 1.6 %pick.1 = bf16[8,3,16,128]{3,2,1,0:T(8,128)(2,1)} custom-call(s32[8,16]{1,0:T(8,128)S(1)} %bitcast.17, bf16[64,56,128]{2,1,0:T(8,128)(2,1)S(1)} %all-to-all-done.1.got_ref), custom_call_target="tpu_custom_call" | custom-call | tf_op jit(solution)/shard_map/pick/pallas_call | solution.py:194
  62.7 3.4 %all-to-all-start.2 = ((bf16[8,3,16,128]{3,2,1,0:T(8,128)(2,1)}), bf16[8,3,16,128]{3,2,1,0:T(8,128)(2,1)S(1)}, u32[]{:S(2)}, u32[]{:S(2)}) async-start(bf16[8,3,16,128]{3,2,1,0:T(8,128)(2,1)} %pick.1), calls=%async_computation.2 | async-start | bytes 196608 | tf_op jit(solution)/shard_map/all_to_all | solution.py:206
  66.1 0.2 multiply_convert_fusion
  66.4 1.0 convert_element_type.73.ta_ref
  67.4 5.0 %all-to-all-done.2.pick_ref = bf16[8,3,16,128]{3,2,1,0:T(8,128)(2,1)S(1)} async-done(((bf16[8,3,16,128]{3,2,1,0:T(8,128)(2,1)}), bf16[8,3,16,128]{3,2,1,0:T(8,128)(2,1)S(1)}, u32[]{:S(2)}, u32[]{:S(2)}) %all-to-all-start.2) | async-done | bytes 98336 | tf_op jit(solution)/shard_map/all_to_all | solution.py:206
  72.4 0.0 copy-done.1
  72.4 10.9 %owner.1 = bf16[8,8,32,512]{3,2,1,0:T(8,128)(2,1)S(1)} custom-call(s32[1]{0:T(128)} %bitcast.14.count_ref, bf16[64,56,128]{2,1,0:T(8,128)(2,1)S(1)} %all-to-all-done.1.got_ref, bf16[8,3,16,128]{3,2,1,0:T(8,128)(2,1)S(1)} %all-to-all-done.2.pick_ref, f32[1,128]{1,0:T(1,128)S(1)} %copy-done.1, bf16[256,256]{1,0:T(8,128)(2,1)S(1)} %bitcast.15, ...), custom_call_target="tpu_custom_call" | custom-call | tf_op jit(solution)/shard_map/owner/pallas_call | solution.py:210
  83.3 30.9 %all_to_all.25 = bf16[8,8,32,512]{3,2,1,0:T(8,128)(2,1)S(1)} all-to-all(bf16[8,8,32,512]{3,2,1,0:T(8,128)(2,1)S(1)} %owner.1), channel_id=1, replica_groups=mesh['ka'=8,'yh'=4,'yl'=2,'zh'=2,'x'=4] {'yl','x'}, dimensions={0} | all-to-all | bytes 4194304 | tf_op jit(solution)/shard_map/all_to_all | solution.py:225
  114.3 0.4 reduce_sum.21
  114.7 18.2 %all_to_all.26 = bf16[8,32,512]{2,1,0:T(8,128)(2,1)S(1)} all-to-all(bf16[8,32,512]{2,1,0:T(8,128)(2,1)S(1)} %reduce_sum.21), channel_id=1, replica_groups=mesh['ka'=8,'yh'=4,'yl'=2,'zh'=2,'x'=4] {'yh','zh'}, dimensions={0} | all-to-all | bytes 524288 | tf_op jit(solution)/shard_map/all_to_all | solution.py:227
  132.9 0.7 convert_reduce_fusion
  (6 shorter events, 0.1 us)
Async XLA Ops:
  3.2 13.0 %all-to-all-start = ((f32[8,8,128]{2,1,0:T(8,128)}), f32[8,8,128]{2,1,0:T(8,128)S(1)}, u32[]{:S(2)}, u32[]{:S(2)}) async-start(f32[8,8,128]{2,1,0:T(8,128)} %piece.1), calls=%async_computation | async-start | bytes 65536 | tf_op jit(solution)/shard_map/all_to_all | solution.py:173
  10.5 1.0 copy-start
  17.3 43.8 %all-to-all-start.1 = ((bf16[64,56,128]{2,1,0:T(8,128)(2,1)}), bf16[64,56,128]{2,1,0:T(8,128)(2,1)S(1)}, u32[]{:S(2)}, u32[]{:S(2)}) async-start(bf16[64,56,128]{2,1,0:T(8,128)(2,1)} %pack.1), calls=%async_computation.1 | async-start | bytes 1835008 | tf_op jit(solution)/shard_map/all_to_all | solution.py:192
  33.5 38.9 %copy-start.1 = (f32[1,128]{1,0:T(1,128)S(1)}, f32[1,128]{1,0:T(1,128)}, u32[]{:S(2)}) copy-start(f32[1,128]{1,0:T(1,128)} %e_cond_ref.1) | copy-start | bytes 1540
  62.7 9.6 %all-to-all-start.2 = ((bf16[8,3,16,128]{3,2,1,0:T(8,128)(2,1)}), bf16[8,3,16,128]{3,2,1,0:T(8,128)(2,1)S(1)}, u32[]{:S(2)}, u32[]{:S(2)}) async-start(bf16[8,3,16,128]{3,2,1,0:T(8,128)(2,1)} %pick.1), calls=%async_computation.2 | async-start | bytes 196608 | tf_op jit(solution)/shard_map/all_to_all | solution.py:206

commit v8 on v7

--- a/solution.py
+++ b/solution.py
@@ -95,17 +95,12 @@
     out_ref[...] = picked_s[...].astype(bf16)
 
 
-def owner_kernel(count_ref, got_ref, pick_ref, e_cond_ref, bd_ref, ta_ref, out_ref,
-                 first_s, moved_s, wtd_s, weight_s):
-    live = lax.broadcasted_iota(jnp.int32, (SLOTS, BC), 0) < count_ref[0]
-    e_pick = pick_ref[0, 2].astype(f32)
-    weight_s[...] = jnp.where(live, 1.0, 0.0) * 2.0 / (e_cond_ref[...] - e_pick)
-
+def owner_slots(slots, got_ref, pick_ref, bd_ref, ta_ref, out_ref, first_s, moved_s, wtd_s, weight_s):
     def to_first(i, carry):
         cond = [got_ref[8 * i + t, :OWN, :].astype(f32) for t in range(8)]
         cond = [jnp.concatenate(cond[4 * h:4 * h + 4], axis=0) for h in range(2)]
         pick = [pick_ref[i, h].astype(f32).T for h in range(2)]
-        for s0 in range(0, SLOTS, GROUP):
+        for s0 in range(0, slots, GROUP):
             pair = [
                 jnp.concatenate([cond[h] * pick[h][:, s:s + 1] for h in range(2)], axis=0).astype(bf16)
                 for s in range(s0, s0 + GROUP)
@@ -123,7 +118,7 @@
 
     def to_moved(kg, carry):
         start = pl.multiple_of(kg * 256, 256)
-        for s0 in range(0, SLOTS, GROUP):
+        for s0 in range(0, slots, GROUP):
             lanes = slice(s0 * BC, (s0 + GROUP) * BC)
             moved = jnp.dot(ta_ref[...], first_s[pl.ds(start, 256), lanes], preferred_element_type=f32)
             moved = moved.astype(bf16)
@@ -143,7 +138,7 @@
     def to_out(i, carry):
         start = pl.multiple_of(i * 256, 256)
         total = lax.dot_general(
-            moved_s[pl.ds(start, 256), :], wtd_s[...], (((1,), (1,)), ((), ())),
+            moved_s[pl.ds(start, 256), :slots * BC], wtd_s[:, :slots * BC], (((1,), (1,)), ((), ())),
             preferred_element_type=f32,
         )
         total = (total * (2.0 / (SLOTS * BC * N_PAIR))).astype(bf16)
@@ -154,6 +149,21 @@
         return carry
 
     lax.fori_loop(0, 8, to_out, 0, unroll=4)
+
+
+def owner_kernel(count_ref, got_ref, pick_ref, e_cond_ref, bd_ref, ta_ref, out_ref,
+                 first_s, moved_s, wtd_s, weight_s):
+    count = count_ref[0]
+    live = lax.broadcasted_iota(jnp.int32, (SLOTS, BC), 0) < count
+    e_pick = pick_ref[0, 2].astype(f32)
+    weight_s[...] = jnp.where(live, 1.0, 0.0) * 2.0 / (e_cond_ref[...] - e_pick)
+
+    groups = jnp.clip(lax.div(count + GROUP - 1, GROUP), 1, SLOTS // GROUP)
+    for slots in range(GROUP, SLOTS + GROUP, GROUP):
+        @pl.when(groups * GROUP == slots)
+        def _(slots=slots):
+            owner_slots(slots, got_ref, pick_ref, bd_ref, ta_ref, out_ref,
+                        first_s, moved_s, wtd_s, weight_s)
 
 
 def shards(cond_orbitals, cond_energy, val_orbitals, val_energy, val_slots, owner_count):

time: 134 us -> 134 us (level)
  Pallas kernels: 15.7 us -> 13.6 us
  blocking collectives: 49.2 us -> 50.9 us
    pallas_call x1, Pallas kernels: 10.9 us -> 8.86 us  [shards(): pl.pallas_call(owner_kernel, out_shape=jax.ShapeDtypeStruct((N_YL * N_X,...]
    all_to_all x1, blocking collectives: 18.2 us -> 19.6 us  [shards(): part = lax.all_to_all(part, FAR, 0, 0, tiled=True)]
where the time goes in v8:
time: 134 us; the launch traced here: 133 us
  blocking collectives  50.9 us (38%)
  waiting for transfers between devices  36 us (27%)
  starting transfers between devices  26.8 us (20%)
  Pallas kernels  13.6 us (10%)
  local copies, waits for them, and re-layouts  2.66 us (2%)
  other arithmetic  1.81 us (1%)
  between operations  1.43 us (1%)
    all_to_all x1, blocking collectives, shards(): part = lax.all_to_all(part, NEAR, 0, 0, tiled=True)  31.3 us
    all_to_all x1, waiting for transfers between devices, shards(): got = lax.all_to_all(packed, PAIR, 0, 0, tiled=True)  26.4 us
    all_to_all x1, blocking collectives, shards(): part = lax.all_to_all(part, FAR, 0, 0, tiled=True)  19.6 us
    all_to_all x1, starting transfers between devices, shards(): got = lax.all_to_all(packed, PAIR, 0, 0, tiled=True)  16.2 us
    pallas_call x1, Pallas kernels, shards(): pl.pallas_call(owner_kernel, out_shape=jax.ShapeDtypeStruct((N_YL * N_X,...  8.86 us
    all_to_all x1, starting transfers between devices, shards(): pieces = lax.all_to_all(pieces, 'ka', 0, 0, tiled=True)  7.28 us
    all_to_all x1, waiting for transfers between devices, shards(): picked = lax.all_to_all(picked, 'ka', 0, 0, tiled=True)  5.01 us
    all_to_all x1, waiting for transfers between devices, shards(): pieces = lax.all_to_all(pieces, 'ka', 0, 0, tiled=True)  4.61 us
  transfers between devices with their start and end apart: 3, of which 3 were waited for; matrix products, arithmetic and copies ran while one was open for 1% of the time, Pallas kernels for 0%

profile of v8, /device:TPU:16, one launch (start us, length us, event | category | flops | bytes accessed | tf_op | source)
XLA Modules:
  0.0 133.2 jit_solution(9015022123981595176)
XLA Ops:
  0.7 0.6 broadcast_in_dim.40.energy_ref
  1.2 2.0 %piece.1 = f32[8,8,128]{2,1,0:T(8,128)} custom-call(bf16[8,128]{1,0:T(8,128)(2,1)} %broadcast_in_dim.40.energy_ref, bf16[1,2048]{1,0:T(2,128)(2,1)} %val_ref.1, s32[1,16]{1,0:T(1,128)} %bitcast.19), custom_call_target="tpu_custom_call" | custom-call | tf_op jit(solution)/shard_map/piece/pallas_call | solution.py:170
  3.2 7.3 %all-to-all-start = ((f32[8,8,128]{2,1,0:T(8,128)}), f32[8,8,128]{2,1,0:T(8,128)S(1)}, u32[]{:S(2)}, u32[]{:S(2)}) async-start(f32[8,8,128]{2,1,0:T(8,128)} %piece.1), calls=%async_computation | async-start | bytes 65536 | tf_op jit(solution)/shard_map/all_to_all | solution.py:183
  10.5 0.0 copy-start
  10.5 1.0 copy-done
  11.6 0.1 cond.1.cond_ref
  11.7 4.6 %all-to-all-done.pieces_ref = f32[8,8,128]{2,1,0:T(8,128)S(1)} async-done(((f32[8,8,128]{2,1,0:T(8,128)}), f32[8,8,128]{2,1,0:T(8,128)S(1)}, u32[]{:S(2)}, u32[]{:S(2)}) %all-to-all-start) | async-done | bytes 32800 | tf_op jit(solution)/shard_map/all_to_all | solution.py:183
  16.3 1.0 pack.1
  17.3 16.2 %all-to-all-start.1 = ((bf16[64,56,128]{2,1,0:T(8,128)(2,1)}), bf16[64,56,128]{2,1,0:T(8,128)(2,1)S(1)}, u32[]{:S(2)}, u32[]{:S(2)}) async-start(bf16[64,56,128]{2,1,0:T(8,128)(2,1)} %pack.1), calls=%async_computation.1 | async-start | bytes 1835008 | tf_op jit(solution)/shard_map/all_to_all | solution.py:202
  33.5 0.0 copy-start.1
  34.2 0.2 fusion
  34.4 0.2 multiply_convert_fusion.1
  34.6 0.1 fusion.2
  34.7 26.4 %all-to-all-done.1.got_ref = bf16[64,56,128]{2,1,0:T(8,128)(2,1)S(1)} async-done(((bf16[64,56,128]{2,1,0:T(8,128)(2,1)}), bf16[64,56,128]{2,1,0:T(8,128)(2,1)S(1)}, u32[]{:S(2)}, u32[]{:S(2)}) %all-to-all-start.1) | async-done | bytes 917536 | tf_op jit(solution)/shard_map/all_to_all | solution.py:202
  61.1 1.6 %pick.1 = bf16[8,3,16,128]{3,2,1,0:T(8,128)(2,1)} custom-call(s32[8,16]{1,0:T(8,128)S(1)} %bitcast.17, bf16[64,56,128]{2,1,0:T(8,128)(2,1)S(1)} %all-to-all-done.1.got_ref), custom_call_target="tpu_custom_call" | custom-call | tf_op jit(solution)/shard_map/pick/pallas_call | solution.py:204
  62.7 3.4 %all-to-all-start.2 = ((bf16[8,3,16,128]{3,2,1,0:T(8,128)(2,1)}), bf16[8,3,16,128]{3,2,1,0:T(8,128)(2,1)S(1)}, u32[]{:S(2)}, u32[]{:S(2)}) async-start(bf16[8,3,16,128]{3,2,1,0:T(8,128)(2,1)} %pick.1), calls=%async_computation.2 | async-start | bytes 196608 | tf_op jit(solution)/shard_map/all_to_all | solution.py:216
  66.1 0.2 multiply_convert_fusion
  66.4 1.0 convert_element_type.73.ta_ref
  67.4 5.0 %all-to-all-done.2.pick_ref = bf16[8,3,16,128]{3,2,1,0:T(8,128)(2,1)S(1)} async-done(((bf16[8,3,16,128]{3,2,1,0:T(8,128)(2,1)}), bf16[8,3,16,128]{3,2,1,0:T(8,128)(2,1)S(1)}, u32[]{:S(2)}, u32[]{:S(2)}) %all-to-all-start.2) | async-done | bytes 98336 | tf_op jit(solution)/shard_map/all_to_all | solution.py:216
  72.4 0.0 copy-done.1
  72.4 8.9 %owner.1 = bf16[8,8,32,512]{3,2,1,0:T(8,128)(2,1)S(1)} custom-call(s32[1]{0:T(128)} %bitcast.14.count_ref, bf16[64,56,128]{2,1,0:T(8,128)(2,1)S(1)} %all-to-all-done.1.got_ref, bf16[8,3,16,128]{3,2,1,0:T(8,128)(2,1)S(1)} %all-to-all-done.2.pick_ref, f32[1,128]{1,0:T(1,128)S(1)} %copy-done.1, bf16[256,256]{1,0:T(8,128)(2,1)S(1)} %bitcast.15, ...), custom_call_target="tpu_custom_call" | custom-call | tf_op jit(solution)/shard_map/owner/pallas_call | solution.py:220
  81.3 31.3 %all_to_all.25 = bf16[8,8,32,512]{3,2,1,0:T(8,128)(2,1)S(1)} all-to-all(bf16[8,8,32,512]{3,2,1,0:T(8,128)(2,1)S(1)} %owner.1), channel_id=1, replica_groups=mesh['ka'=8,'yh'=4,'yl'=2,'zh'=2,'x'=4] {'yl','x'}, dimensions={0} | all-to-all | bytes 4194304 | tf_op jit(solution)/shard_map/all_to_all | solution.py:235
  112.5 0.4 reduce_sum.21
  112.9 19.6 %all_to_all.26 = bf16[8,32,512]{2,1,0:T(8,128)(2,1)S(1)} all-to-all(bf16[8,32,512]{2,1,0:T(8,128)(2,1)S(1)} %reduce_sum.21), channel_id=1, replica_groups=mesh['ka'=8,'yh'=4,'yl'=2,'zh'=2,'x'=4] {'yh','zh'}, dimensions={0} | all-to-all | bytes 524288 | tf_op jit(solution)/shard_map/all_to_all | solution.py:237
  132.6 0.7 convert_reduce_fusion
  (6 shorter events, 0.1 us)
Async XLA Ops:
  3.2 13.0 %all-to-all-start = ((f32[8,8,128]{2,1,0:T(8,128)}), f32[8,8,128]{2,1,0:T(8,128)S(1)}, u32[]{:S(2)}, u32[]{:S(2)}) async-start(f32[8,8,128]{2,1,0:T(8,128)} %piece.1), calls=%async_computation | async-start | bytes 65536 | tf_op jit(solution)/shard_map/all_to_all | solution.py:183
  10.5 1.0 copy-start
  17.3 43.8 %all-to-all-start.1 = ((bf16[64,56,128]{2,1,0:T(8,128)(2,1)}), bf16[64,56,128]{2,1,0:T(8,128)(2,1)S(1)}, u32[]{:S(2)}, u32[]{:S(2)}) async-start(bf16[64,56,128]{2,1,0:T(8,128)(2,1)} %pack.1), calls=%async_computation.1 | async-start | bytes 1835008 | tf_op jit(solution)/shard_map/all_to_all | solution.py:202
  33.5 38.9 %copy-start.1 = (f32[1,128]{1,0:T(1,128)S(1)}, f32[1,128]{1,0:T(1,128)}, u32[]{:S(2)}) copy-start(f32[1,128]{1,0:T(1,128)} %e_cond_ref.1) | copy-start | bytes 1540
  62.7 9.6 %all-to-all-start.2 = ((bf16[8,3,16,128]{3,2,1,0:T(8,128)(2,1)}), bf16[8,3,16,128]{3,2,1,0:T(8,128)(2,1)S(1)}, u32[]{:S(2)}, u32[]{:S(2)}) async-start(bf16[8,3,16,128]{3,2,1,0:T(8,128)(2,1)} %pick.1), calls=%async_computation.2 | async-start | bytes 196608 | tf_op jit(solution)/shard_map/all_to_all | solution.py:216
